TPU v7x, 256 devices: a whole 4x4x8 slice. The times are simulated.
256 devices in a mesh: dp: 8 (over z_hi, x), mx: 4 (over z_lo), my: 8 (over y, core).
Axes of the slice: x: 4, y: 4, z: 8 (z_hi: 2, z_lo: 4; z = z_hi * 4 + z_lo), core: 2. Of those that a mesh axis runs over, the one named last changes fastest.
Arguments:
- tokens: bfloat16 [4096, 6144], P('dp', ('my', 'mx')), may hold values from -6 to 6
- w_in: bfloat16 [6144, 12288], P('my', 'mx'), may hold values from -0.078125 to 0.078125
- w_out: bfloat16 [12288, 6144], P('mx', 'my'), may hold values from -0.0546875 to 0.0546875
- cotangent: bfloat16 [4096, 6144], P('dp', ('my', 'mx')), may hold values from -6 to 6
Outputs:
- mixed: bfloat16 [4096, 6144], P('dp', ('my', 'mx'))
- d_tokens: bfloat16 [4096, 6144], P('dp', ('my', 'mx'))
- grad_in: bfloat16 [6144, 12288], P('my', ('mx', 'dp'))
- grad_out: bfloat16 [12288, 6144], P(('mx', 'dp'), 'my')
All inputs are finite; a program needn't handle non-finite values.
Results may differ from a plain program's by a relative error of at most 0.0049.
Values may be sent and summed in bfloat16 or wider, within the bound.
A program may use at most 128 MiB of HBM per device.

v0:
```python
import jax
import jax.numpy as jnp
from jax import lax
from jax.sharding import PartitionSpec as P


def gelu_parts(pre_act):
    root_half = 0.7071067811865476
    inv_root_two_pi = 0.3989422804014327
    cumul = 0.5 * (1.0 + lax.erf(pre_act * root_half))
    value = pre_act * cumul
    derivative = cumul + pre_act * jnp.exp(-0.5 * pre_act * pre_act) * inv_root_two_pi
    return (value, derivative)


def rows_product(left, right):
    return lax.dot_general(
        left, right, (((0,), (0,)), ((), ())), preferred_element_type=jnp.float32
    )


def cols_product(left, right):
    return lax.dot_general(
        left, right, (((1,), (1,)), ((), ())), preferred_element_type=jnp.float32
    )


def per_device(tokens, w_in, w_out, cotangent):
    features = lax.all_gather(tokens, "mx", axis=1, tiled=True)
    fwd_part = jnp.dot(features, w_in, preferred_element_type=jnp.float32)
    pre_act = lax.psum_scatter(fwd_part, "my", scatter_dimension=1, tiled=True)
    value, derivative = gelu_parts(pre_act)
    hidden = value.astype(jnp.bfloat16)
    hidden_all = lax.all_gather(hidden, "my", axis=1, tiled=True)
    out_part = jnp.dot(hidden_all, w_out, preferred_element_type=jnp.float32)
    mixed = lax.psum_scatter(out_part, "mx", scatter_dimension=1, tiled=True).astype(jnp.bfloat16)
    cot_all = lax.all_gather(cotangent, "mx", axis=1, tiled=True)
    back_part = cols_product(cot_all, w_out)
    d_hidden = lax.psum_scatter(back_part, "my", scatter_dimension=1, tiled=True)
    grad_pre = (d_hidden * derivative).astype(jnp.bfloat16)
    grad_pre_all = lax.all_gather(grad_pre, "my", axis=1, tiled=True)
    input_part = cols_product(grad_pre_all, w_in)
    d_tokens = lax.psum_scatter(input_part, "mx", scatter_dimension=1, tiled=True).astype(
        jnp.bfloat16
    )
    local_in = rows_product(features, grad_pre_all)
    local_out = rows_product(hidden_all, cot_all)
    summed_in, summed_out = (
        lax.psum_scatter(local_in, "dp", scatter_dimension=1, tiled=True),
        lax.psum_scatter(local_out, "dp", scatter_dimension=0, tiled=True),
    )
    grad_in = summed_in.astype(jnp.bfloat16)
    grad_out = summed_out.astype(jnp.bfloat16)
    return (mixed, d_tokens, grad_in, grad_out)


def solution(mesh):
    placed = (P("dp", ("my", "mx")), P("my", "mx"), P("mx", "my"), P("dp", ("my", "mx")))
    return jax.shard_map(
        per_device,
        mesh=mesh,
        in_specs=placed,
        out_specs=(
            P("dp", ("my", "mx")),
            P("dp", ("my", "mx")),
            P("my", ("mx", "dp")),
            P(("mx", "dp"), "my"),
        ),
        check_vma=False,
    )
```

profile of v0, /device:TPU:1, one launch (start us, length us, event | category | flops | bytes accessed | tf_op | source)
XLA Modules:
  0.0 695.2 jit_solution(6945484912618450182)
XLA Ops:
  7.2 0.0 reduce-scatter.11.cloned.1.call-start
  7.2 19.3 %all_gather.14 = bf16[512,768]{0,1:T(8,128)(2,1)S(1)} all-gather(bf16[512,192]{0,1:T(8,128)(2,1)} %param.7), channel_id=1, replica_groups=mesh['dp'=8,'mx'=4,'my'=8] {'mx'}, dimensions={1}, use_global_device_ids=true | all-gather | bytes 983040 | tf_op jit(solution)/shard_map/all_gather | solution.py:37
  26.5 6.9 fusion.8
  33.4 0.0 copy-start
  33.4 0.0 reduce-scatter.11.cloned.1.call-update
  33.4 0.0 reduce-scatter.7.cloned.1.call-start
  33.5 0.9 copy-done
  34.3 16.6 %all_gather.12 = bf16[512,768]{0,1:T(8,128)(2,1)S(1)} all-gather(bf16[512,192]{0,1:T(8,128)(2,1)S(1)} %copy-done), channel_id=1, replica_groups=mesh['dp'=8,'mx'=4,'my'=8] {'mx'}, dimensions={1}, use_global_device_ids=true | all-gather | bytes 983040 | tf_op jit(solution)/shard_map/all_gather | solution.py:29
  50.9 6.9 fusion.6
  57.8 0.0 reduce-scatter.7.cloned.1.call-update
  57.8 0.0 all-gather.3.cloned.1.call-start
  57.9 23.1 %reduce-scatter.11.cloned.1.call-done = f32[512,384]{1,0:T(8,128)} async-done(((f32[512,3072]{1,0:T(8,128)}), f32[512,384]{1,0:T(8,128)}) %reduce-scatter.11.cloned.1.call-update) | async-done | bytes 786448 | tf_op jit(solution)/shard_map/reduce_scatter | solution.py:39
  81.0 47.4 %reduce-scatter.7.cloned.1.call-done = f32[512,384]{1,0:T(8,128)} async-done(((f32[512,3072]{1,0:T(8,128)}), f32[512,384]{1,0:T(8,128)}) %reduce-scatter.7.cloned.1.call-update) | async-done | bytes 786448 | tf_op jit(solution)/shard_map/reduce_scatter | solution.py:31
  128.4 2.6 fusion.5
  131.0 0.0 all-gather.3.cloned.1.call-update
  131.0 0.0 all-gather.5.cloned.1.call-start
  131.1 0.5 all-gather.5.cloned.1.call-update
  131.6 0.0 reduce-scatter.9.cloned.1.call-start
  131.6 30.5 %all-gather.3.cloned.1.call-done = bf16[512,3072]{1,0:T(8,128)(2,1)} async-done(((bf16[512,384]{1,0:T(8,128)(2,1)}), bf16[512,3072]{1,0:T(8,128)(2,1)}) %all-gather.3.cloned.1.call-update) | async-done | bytes 3145744 | tf_op jit(solution)/shard_map/all_gather | solution.py:34
  162.2 7.1 %fusion.7 = f32[512,768]{0,1:T(8,128)} fusion(bf16[512,3072]{1,0:T(8,128)(2,1)} %all-gather.3.cloned.1.call-done, bf16[3072,768]{1,0:T(8,128)(2,1)} %param.6), kind=kOutput, calls=%fused_computation.11 | convolution fusion | flops 2415919104 | bytes 9437184 | tf_op jit(solution)/shard_map/dot_general | solution.py:35
  169.3 0.0 reduce-scatter.9.cloned.1.call-update
  169.3 0.0 reduce-scatter.13.cloned.1.call-start
  169.4 25.4 %all-gather.5.cloned.1.call-done = bf16[512,3072]{1,0:T(8,128)(2,1)} async-done(((bf16[512,384]{1,0:T(8,128)(2,1)}), bf16[512,3072]{1,0:T(8,128)(2,1)}) %all-gather.5.cloned.1.call-update) | async-done | bytes 3145744 | tf_op jit(solution)/shard_map/all_gather | solution.py:41
  194.8 7.1 %fusion.9 = f32[512,768]{0,1:T(8,128)} fusion(bf16[512,3072]{1,0:T(8,128)(2,1)} %all-gather.5.cloned.1.call-done, bf16[768,3072]{1,0:T(8,128)(2,1)} %param.5), kind=kOutput, calls=%fused_computation.13 | convolution fusion | flops 2415919104 | bytes 9437184 | tf_op jit(solution)/shard_map/dot_general | solution.py:23
  201.9 0.0 reduce-scatter.13.cloned.1.call-update
  201.9 0.0 reduce-scatter.15.cloned.1.call-start
  202.0 8.2 %convolution_bitcast_fusion = f32[768,3072]{0,1:T(8,128)} fusion(bf16[512,3072]{1,0:T(8,128)(2,1)} %all-gather.5.cloned.1.call-done, bf16[512,768]{0,1:T(8,128)(2,1)S(1)} %all_gather.12), kind=kOutput, calls=%fused_computation | convolution fusion | flops 2415919104 | bytes 13369344 | tf_op jit(solution)/shard_map/dot_general | solution.py:17
  210.2 0.0 reduce-scatter.15.cloned.1.call-update
  210.2 0.2 reduce-scatter.17.cloned.1.call-start
  210.4 8.2 %fusion.10 = f32[3072,768]{1,0:T(8,128)} fusion(bf16[512,3072]{1,0:T(8,128)(2,1)} %all-gather.3.cloned.1.call-done, bf16[512,768]{0,1:T(8,128)(2,1)S(1)} %all_gather.14), kind=kOutput, calls=%fused_computation.14 | convolution fusion | flops 2415919104 | bytes 13369344 | tf_op jit(solution)/shard_map/dot_general | solution.py:17
  218.7 0.0 reduce-scatter.17.cloned.1.call-update
  218.7 18.6 %reduce-scatter.9.cloned.1.call-done = f32[512,192]{0,1:T(8,128)} async-done(((f32[512,768]{0,1:T(8,128)}), f32[512,192]{0,1:T(8,128)}) %reduce-scatter.9.cloned.1.call-update) | async-done | bytes 393232 | tf_op jit(solution)/shard_map/reduce_scatter | solution.py:36
  237.3 1.7 convert_element_type.19
  239.0 40.5 %reduce-scatter.13.cloned.1.call-done = f32[512,192]{0,1:T(8,128)} async-done(((f32[512,768]{0,1:T(8,128)}), f32[512,192]{0,1:T(8,128)}) %reduce-scatter.13.cloned.1.call-update) | async-done | bytes 393232 | tf_op jit(solution)/shard_map/reduce_scatter | solution.py:43
  279.5 1.7 convert_element_type.21
  281.2 203.4 %reduce-scatter.15.cloned.1.call-done = f32[768,384]{0,1:T(8,128)} async-done(((f32[768,3072]{0,1:T(8,128)}), f32[768,384]{0,1:T(8,128)}) %reduce-scatter.15.cloned.1.call-update) | async-done | bytes 1179664 | tf_op jit(solution)/shard_map/reduce_scatter | solution.py:49
  484.6 1.3 convert_element_type.22
  486.0 1.1 copy.8
  487.0 199.2 %reduce-scatter.17.cloned.1.call-done = f32[384,768]{1,0:T(8,128)} async-done(((f32[3072,768]{1,0:T(8,128)}), f32[384,768]{1,0:T(8,128)}) %reduce-scatter.17.cloned.1.call-update) | async-done | bytes 1179664 | tf_op jit(solution)/shard_map/reduce_scatter | solution.py:50
  686.2 2.1 convert_element_type.23
Async XLA Ops:
  7.2 73.8 %reduce-scatter.11.cloned.1.call-start = ((), (), s32[]{:S(2)}) async-start(), calls=%async_computation.9 | async-start | bytes 7077888 | tf_op jit(solution)/shard_map/reduce_scatter | solution.py:39
  33.4 0.9 copy-start
  33.4 94.9 %reduce-scatter.7.cloned.1.call-start = ((), (), s32[]{:S(2)}) async-start(), calls=%async_computation.6 | async-start | bytes 7077888 | tf_op jit(solution)/shard_map/reduce_scatter | solution.py:31
  57.8 104.3 %all-gather.3.cloned.1.call-start = ((), (), s32[]{:S(2)}) async-start(), calls=%async_computation.7 | async-start | bytes 3538944 | tf_op jit(solution)/shard_map/all_gather | solution.py:34
  131.0 63.8 %all-gather.5.cloned.1.call-start = ((), (), s32[]{:S(2)}) async-start(), calls=%async_computation.10 | async-start | bytes 3538944 | tf_op jit(solution)/shard_map/all_gather | solution.py:41
  131.6 105.7 %reduce-scatter.9.cloned.1.call-start = ((), (), s32[]{:S(2)}) async-start(), calls=%async_computation.8 | async-start | bytes 1966080 | tf_op jit(solution)/shard_map/reduce_scatter | solution.py:36
  169.3 110.2 %reduce-scatter.13.cloned.1.call-start = ((), (), s32[]{:S(2)}) async-start(), calls=%async_computation.11 | async-start | bytes 1966080 | tf_op jit(solution)/shard_map/reduce_scatter | solution.py:43
  201.9 282.7 %reduce-scatter.15.cloned.1.call-start = ((), (), s32[]{:S(2)}) async-start(), calls=%async_computation.12 | async-start | bytes 10616832 | tf_op jit(solution)/shard_map/reduce_scatter | solution.py:49
  210.2 476.1 %reduce-scatter.17.cloned.1.call-start = ((), (), s32[]{:S(2)}) async-start(), calls=%async_computation.13 | async-start | bytes 10616832 | tf_op jit(solution)/shard_map/reduce_scatter | solution.py:50
Sparse Core Ops, SparseCore 0:
  33.6 47.3 reduce-scatter.10
  83.5 44.7 reduce-scatter.6
  131.1 30.9 all-gather.2
  164.4 30.3 all-gather.4
  197.2 40.0 reduce-scatter.8
  239.7 39.7 reduce-scatter.12
  283.7 200.8 reduce-scatter.14
  489.4 196.7 reduce-scatter.16
where the time goes:
time: 696 us; the launch traced here: 695 us
  waiting for transfers between devices  589 us (85%)
  matrix products  44.5 us (6%)
  blocking collectives  35.8 us (5%)
  between operations  14.1 us (2%)
  other arithmetic  9.49 us (1%)
    reduce_scatter x1, waiting for transfers between devices, per_device(): lax.psum_scatter(local_in, 'dp', scatter_dimension=1, tiled=True)  203 us
    reduce_scatter x1, waiting for transfers between devices, per_device(): lax.psum_scatter(local_out, 'dp', scatter_dimension=0, tiled=True)  199 us
    reduce_scatter x1, waiting for transfers between devices, per_device(): pre_act = lax.psum_scatter(fwd_part, 'my', scatter_dimension=1, tiled=True)  47.4 us
    reduce_scatter x1, waiting for transfers between devices, per_device(): lax.psum_scatter(input_part, 'mx', scatter_dimension=1, tiled=True)  40.5 us
    all_gather x1, waiting for transfers between devices, per_device(): hidden_all = lax.all_gather(hidden, 'my', axis=1, tiled=True)  30.5 us
    all_gather x1, waiting for transfers between devices, per_device(): grad_pre_all = lax.all_gather(grad_pre, 'my', axis=1, tiled=True)  25.4 us
    reduce_scatter x1, waiting for transfers between devices, per_device(): lax.psum_scatter(back_part, 'my', scatter_dimension=1, tiled=True)  23.1 us
    all_gather x1, blocking collectives, per_device(): cot_all = lax.all_gather(cotangent, 'mx', axis=1, tiled=True)  19.3 us
  transfers between devices with their start and end apart: 8, of which 8 were waited for; matrix products, arithmetic and copies ran while one was open for 6% of the time, Pallas kernels for 0%

commit v1 on v0

v1 whole, which is shorter than its diff:
```python
import jax
import jax.numpy as jnp
from jax import lax
from jax.experimental import pallas as pl
from jax.experimental.pallas import tpu as pltpu
from jax.sharding import Mesh
from jax.sharding import PartitionSpec as P

MESH = pl.DeviceIdType.MESH
BF = jnp.bfloat16
F32 = jnp.float32

TASKS = (
    (0, 0, 0, 3),
    (0, 1, 0, 3),
    (1, 0, 0, 3),
    (1, 1, 0, 1),
    (1, 1, 1, 1),
    (1, 1, 2, 1),
)
LINKS = {"y+": (0.0244, 2.4), "y-": (0.0244, 2.4), "x+": (0.0244, 2.4), "x-": (0.0244, 2.4)}
LINKS.update({"z+": (0.0244, 2.4), "z-": (0.0244, 2.4), "c": (0.0037, 0.9)})


def gelu_parts(pre_act):
    root_half = 0.7071067811865476
    inv_root_two_pi = 0.3989422804014327
    cumul = 0.5 * (1.0 + lax.erf(pre_act * root_half))
    value = pre_act * cumul
    derivative = cumul + pre_act * jnp.exp(-0.5 * pre_act * pre_act) * inv_root_two_pi
    return (value, derivative)


def dot(left, right, dims):
    return lax.dot_general(left, right, ((dims[:1], dims[1:]), ((), ())), preferred_element_type=F32)


class Plan:
    def __init__(self):
        self.steps, self.copies = {}, {}

    def copy(self, name, link, kb, src, dst, landing):
        self.copies[name] = (link, kb, src, dst, landing)

    def step(self, name, needs, cost, body, sends=()):
        self.steps[name] = (tuple(needs), cost, body, tuple(sends))

    def order(self):
        started_by = {c: s for s, v in self.steps.items() for c in v[3]}
        users = {s: [] for s in self.steps}
        for s, (needs, _, _, _) in self.steps.items():
            for n in needs:
                if n in self.copies:
                    link, kb = self.copies[n][:2]
                    per_kb, latency = LINKS[link]
                    users[started_by[n]].append((s, latency + per_kb * kb))
                else:
                    users[n].append((s, 0.0))
        level = {}

        def height(s):
            if s not in level:
                level[s] = self.steps[s][1] + max([height(u) + d for u, d in users[s]], default=0.0)
            return level[s]

        now, done, free = 0.0, {}, {}
        todo, result = list(self.steps), []
        while todo:
            best = None
            for s in todo:
                if any(n not in done for n in self.steps[s][0]):
                    continue
                at = max([done[n] for n in self.steps[s][0]], default=0.0)
                key = (max(at, now), -height(s))
                if best is None or key < best[0]:
                    best = (key, s)
            (at, _), s = best
            now = at + self.steps[s][1]
            done[s] = now
            for c in self.steps[s][3]:
                now += 0.05
                link, kb = self.copies[c][:2]
                per_kb, latency = LINKS[link]
                free[link] = max(free.get(link, 0.0), now) + per_kb * kb
                done[c] = free[link] + latency
            todo.remove(s)
            result.append(s)
        self.estimate = now
        return result


def kernel(tok_in, cot_in, w_in_hbm, w_out_hbm, mix_out, dtok_out, gin_out, gout_out, *scratch):
    (act, w_in, w_out, w_sem, csnd, crcv, own, ysnd, yrcv, deriv, hid, xsnd, xrcv, xown, zacc, zsnd, zrcv, send_sem, recv_sem) = scratch
    zh, x, zl = lax.axis_index("zh"), lax.axis_index("x"), lax.axis_index("zl")
    y, c = lax.axis_index("y"), lax.axis_index("c")
    z = zh * 4 + zl

    def along(axis, by):
        if axis == "z":
            to = lax.rem(z + by + 8, 8)
            return {"zh": to // 4, "zl": lax.rem(to, 4)}
        return {axis: lax.rem(lax.axis_index(axis) + by + 4, 4)}

    targets = {a + s: along(a, 1 if s == "+" else -1) for a in "xyz" for s in "+-"}
    targets["c"] = {"c": 1 - c}

    plan = Plan()

    loads = []
    for j in range(3):
        for xx in range(4):
            at = pl.multiple_of(zh * 1536 + xx * 384 + j * 128, 128)
            part = pl.ds(xx * 128, 128)
            loads.append(pltpu.make_async_copy(w_in_hbm.at[:, pl.ds(at, 128)], w_in.at[j, :, part], w_sem.at[0, j, xx]))
            loads.append(pltpu.make_async_copy(w_out_hbm.at[pl.ds(at, 128), :], w_out.at[j, part, :], w_sem.at[1, j, xx]))
    for load in loads:
        load.start()
    barrier = pltpu.get_barrier_semaphore()
    for target in targets.values():
        pl.semaphore_signal(barrier, inc=1, device_id=target, device_id_type=MESH)
    pl.semaphore_wait(barrier, len(targets))

    def place(a, h, at, first=0, rows=192):
        at = lax.rem(at + 16, 8)
        row = pl.multiple_of(lax.rem(at, 4) * 192 + first, 32)
        return act.at[a, h, pl.ds(row, rows), pl.ds(pl.multiple_of((at // 4) * 256, 256), 256)]

    def gather(a, h):
        source = (tok_in, cot_in)[a]

        def begin():
            place(a, h, z)[...] = source[h]

        for s in range(4):
            for sign, d in ((1, "z+"), (-1, "z-")):
                first, rows = (0, 192) if s < 3 else ((0, 96) if sign == 1 else (96, 96))
                here = place(a, h, z - sign * s, first, rows)
                there = place(a, h, z - sign * (s + 1), first, rows)
                plan.copy(("g", a, h, s, d), d, rows * 0.5, here, here, there)
            needs = [("g", a, h, s - 1, d) for d in ("z+", "z-")] if s else []
            sends = [("g", a, h, s, d) for d in ("z+", "z-")]
            plan.step(("g", a, h, s), needs, 0.1, begin if s == 0 else None, sends)
        plan.step(("act", a, h), [("g", a, h, 3, d) for d in ("z+", "z-")], 0.0, None)

    for a in range(2):
        for h in range(2):
            gather(a, h)

    def wait_weights():
        for load in loads:
            load.wait()

    plan.step("weights", [("g", 0, 0, 2)], 0.1, wait_weights)

    def hidden_task(t):
        p, h, j0, nj = TASKS[t]
        js = range(j0, j0 + nj)
        cut = pl.ds(j0, nj)

        def product(j, row):
            if p == 0:
                return dot(w_in[j, :, pl.ds(row, 128)], act[0, h], (0, 0))
            return dot(w_out[j, pl.ds(row, 128), :], act[1, h], (1, 0))

        def other_half():
            def body(i, _):
                j, k = j0 + i // 2, lax.rem(i, 2)
                row = pl.multiple_of((1 - c) * 256 + k * 128, 128)
                csnd[p, h, j, pl.ds(pl.multiple_of(k * 128, 128), 128), :] = product(j, row).astype(BF)
                return 0

            lax.fori_loop(0, 2 * nj, body, 0)

        def own_half():
            def body(i, _):
                j, k = j0 + i // 2, lax.rem(i, 2)
                row = pl.multiple_of(c * 256 + k * 128, 128)
                own[h, j, pl.ds(pl.multiple_of(k * 128, 128), 128), :] = product(j, row)
                return 0

            lax.fori_loop(0, 2 * nj, body, 0)

        def mine(j, rel, half):
            row = pl.ds(pl.multiple_of(lax.rem(y + rel, 4) * 64 + half * 32, 32), 32)
            return own[h, j, row, :] + crcv[p, h, j, row, :].astype(F32)

        def first_sums():
            for j in js:
                for rel, half in ((2, 0), (2, 1), (1, 1), (3, 0)):
                    ysnd[p, h, j, rel - 1, half] = mine(j, rel, half).astype(BF)

        def relay_sums():
            for j in js:
                for rel, half in ((1, 0), (3, 1)):
                    total = mine(j, rel, half) + yrcv[p, h, j, 1, half].astype(F32)
                    ysnd[p, h, j, rel - 1, half] = total.astype(BF)

        def activate():
            for j in js:
                for half in range(2):
                    total = mine(j, 0, half) + yrcv[p, h, j, 0, half].astype(F32) + yrcv[p, h, j, 2, half].astype(F32)
                    keep = pl.ds(half * 32, 32)
                    if p == 0:
                        value, slope = gelu_parts(total)
                        deriv[h, j, keep, :] = slope
                    else:
                        value = total * deriv[h, j, keep, :]
                    row = pl.ds(pl.multiple_of(c * 256 + y * 64 + half * 32, 32), 32)
                    hid[p, h, j, row, :] = value.astype(BF)

        def piece(core, rel, first=0, rows=64):
            row = core * 256 + lax.rem(y + rel, 4) * 64 + first
            return hid.at[p, h, cut, pl.ds(pl.multiple_of(row, 32), rows), :]

        n = lambda *rest: ("h", t) + rest
        plan.copy(n("c"), "c", 256 * nj, csnd.at[p, h, cut], crcv.at[p, h, cut], crcv.at[p, h, cut])
        for rel, half, d in ((2, 0, "y+"), (2, 1, "y-"), (1, 1, "y+"), (3, 0, "y-"), (1, 0, "y+"), (3, 1, "y-")):
            src, dst = ysnd.at[p, h, cut, rel - 1, half], yrcv.at[p, h, cut, rel - 1, half]
            plan.copy(n("r", rel, half), d, 32 * nj, src, dst, dst)
        needs = [("act", p, h), "weights"] + ([n0 for n0 in fwd_done if p == 1])
        plan.step(n("other"), needs, 0.25 * nj, other_half, [n("c")])
        plan.step(n("own"), [n("other")], 0.25 * nj, own_half)
        plan.step(n("first"), [n("own"), n("c")], 0.15 * nj, first_sums, [n("r", 2, 0), n("r", 2, 1), n("r", 1, 1), n("r", 3, 0)])
        plan.step(n("relay"), [n("first"), n("r", 2, 0), n("r", 2, 1)], 0.1 * nj, relay_sums, [n("r", 1, 0), n("r", 3, 1)])
        plan.copy(n("a", "+"), "y+", 64 * nj, piece(c, 0), piece(c, 0), piece(c, 3))
        plan.copy(n("a", "-"), "y-", 64 * nj, piece(c, 0), piece(c, 0), piece(c, 1))
        plan.copy(n("f", "+"), "y+", 32 * nj, piece(c, 3, 0, 32), piece(c, 3, 0, 32), piece(c, 2, 0, 32))
        plan.copy(n("f", "-"), "y-", 32 * nj, piece(c, 1, 32, 32), piece(c, 1, 32, 32), piece(c, 2, 32, 32))
        for rel in range(4):
            plan.copy(n("k", rel), "c", 64 * nj, piece(c, rel), piece(c, rel), piece(1 - c, rel))
        plan.step(n("act"), [n("relay")] + [n("r", *k) for k in ((1, 1), (3, 0), (1, 0), (3, 1))], 0.2 * nj, activate, [n("a", "+"), n("a", "-"), n("k", 0)])
        plan.step(n("pass"), [n("a", "+"), n("a", "-")], 0.05, None, [n("f", "+"), n("f", "-"), n("k", 1), n("k", 3)])
        plan.step(n("last"), [n("f", "+"), n("f", "-")], 0.05, None, [n("k", 2)])
        plan.step(n("done"), [n("k", rel) for rel in range(4)], 0.0, None)

    fwd_done = []
    for t, task in enumerate(TASKS):
        if task[0] == 0:
            hidden_task(t)
    fwd_done = [("h", t, "act") for t, task in enumerate(TASKS) if task[0] == 0]
    for t, task in enumerate(TASKS):
        if task[0] == 1:
            hidden_task(t)

    def gradient(p, j):
        other = 1 - p
        slot = p * 3 + j

        def product(rel):
            row = pl.ds(pl.multiple_of(lax.rem(x + rel, 4) * 128, 128), 128)
            return sum(dot(hid[p, h, j, row, :], act[other, h], (1, 1)) for h in range(2))

        def multiply():
            def body(i, _):
                total = product(3 - i).astype(BF)
                xsnd[slot, 2 - i, 0] = total[:64]
                xsnd[slot, 2 - i, 1] = total[64:]
                return 0

            lax.fori_loop(0, 3, body, 0)

        def multiply_own():
            xown[slot] = product(0)

        def relay_sums():
            for rel, half in ((1, 0), (3, 1)):
                total = xsnd[slot, rel - 1, half].astype(F32) + xrcv[slot, 1, half].astype(F32)
                xsnd[slot, rel - 1, half] = total.astype(BF)

        def finish():
            for half in range(2):
                rows = pl.ds(half * 64, 64)
                xown[slot, rows, :] = xown[slot, rows, :] + xrcv[slot, 0, half].astype(F32) + xrcv[slot, 2, half].astype(F32)
            if p == 0:
                gout_out[pl.ds(j * 128, 128), :] = xown[slot].astype(BF)
            else:
                gin_out[:, pl.ds(j * 128, 128)] = xown[slot].T.astype(BF)

        n = lambda *rest: ("w", p, j) + rest
        for rel, half, d in ((2, 0, "x+"), (2, 1, "x-"), (1, 1, "x+"), (3, 0, "x-"), (1, 0, "x+"), (3, 1, "x-")):
            plan.copy(n("r", rel, half), d, 96, xsnd.at[slot, rel - 1, half], xrcv.at[slot, rel - 1, half], xrcv.at[slot, rel - 1, half])
        needs = [("act", other, h) for h in range(2)]
        needs += [("h", t, "done") for t, (q, h, j0, nj) in enumerate(TASKS) if q == p and j0 <= j < j0 + nj]
        plan.step(n("mul"), needs, 0.9, multiply, [n("r", 2, 0), n("r", 2, 1), n("r", 1, 1), n("r", 3, 0)])
        plan.step(n("own"), [n("mul")], 0.3, multiply_own)
        plan.step(n("relay"), [n("mul"), n("r", 2, 0), n("r", 2, 1)], 0.15, relay_sums, [n("r", 1, 0), n("r", 3, 1)])
        plan.step(n("end"), [n("own")] + [n("r", *k) for k in ((1, 1), (3, 0), (1, 0), (3, 1))], 0.3, finish)

    for p in range(2):
        for j in range(3):
            gradient(p, j)

    def result(p, h):
        def multiply():
            def body(i, _):
                row = pl.ds(pl.multiple_of(i * 256, 256), 256)
                total = None
                for j in range(3):
                    if p == 0:
                        term = dot(w_out[j, :, row], hid[0, h, j], (0, 0))
                    else:
                        term = dot(w_in[j, row, :], hid[1, h, j], (1, 0))
                    total = term if total is None else total + term
                zacc[p, h, row, :] = total
                return 0

            lax.fori_loop(0, 3, body, 0)

        def mine(rel, first=0, rows=192):
            at = lax.rem(z + rel, 8)
            row = pl.multiple_of(lax.rem(at, 4) * 192 + first, 32)
            return zacc[p, h, pl.ds(row, rows), pl.ds(pl.multiple_of((at // 4) * 256, 256), 256)]

        def first():
            zsnd[p, h, 0, 0, pl.ds(0, 96), :] = mine(4, 0, 96).astype(BF)
            zsnd[p, h, 1, 0, pl.ds(96, 96), :] = mine(4, 96, 96).astype(BF)

        def add(s):
            def body():
                for d, rel in ((0, 4 - s), (1, 4 + s)):
                    for half in range(2):
                        total = mine(rel, half * 96, 96)
                        rows = pl.ds(half * 96, 96)
                        if s > 1 or half == d:
                            total = total + zrcv[p, h, d, s - 1, rows, :].astype(F32)
                        zsnd[p, h, d, s, rows, :] = total.astype(BF)

            return body

        def finish():
            total = mine(0) + zrcv[p, h, 0, 3].astype(F32) + zrcv[p, h, 1, 3].astype(F32)
            (mix_out, dtok_out)[p][h] = total.astype(BF)

        n = lambda *rest: ("z", p, h) + rest
        for d, link in ((0, "z+"), (1, "z-")):
            for s in range(4):
                rows = pl.ds(0, 192) if s else pl.ds(d * 96, 96)
                plan.copy(n("r", s, d), link, 96 if s else 48, zsnd.at[p, h, d, s, rows], zrcv.at[p, h, d, s, rows], zrcv.at[p, h, d, s, rows])
        needs = [("h", t, "done") for t, (q, hh, _, _) in enumerate(TASKS) if q == p and hh == h]
        plan.step(n("mul"), needs, 1.2, multiply)
        plan.step(n(0), [n("mul")], 0.1, first, [n("r", 0, 0), n("r", 0, 1)])
        for s in range(1, 4):
            plan.step(n(s), [n("r", s - 1, 0), n("r", s - 1, 1)], 0.3, add(s), [n("r", s, 0), n("r", s, 1)])
        plan.step(n("end"), [n("r", 3, 0), n("r", 3, 1)], 0.2, finish)

    for p in range(2):
        for h in range(2):
            result(p, h)

    index = {name: i for i, name in enumerate(plan.copies)}
    waited, sent = set(), []

    def remote(name, landing):
        link, _, src, dst, there = plan.copies[name]
        i = index[name]
        src, dst = (there, there) if landing else (src, dst)
        return pltpu.make_async_remote_copy(src, dst, send_sem.at[i], recv_sem.at[i], device_id=targets[link], device_id_type=MESH)

    for name in plan.order():
        needs, _, body, sends = plan.steps[name]
        for need in needs:
            if need in plan.copies and need not in waited:
                remote(need, True).wait_recv()
                waited.add(need)
        if body is not None:
            body()
        for copy in sends:
            remote(copy, False).start()
            sent.append(copy)
    for copy in sent:
        remote(copy, False).wait_send()


def copies_in_all():
    return 32 + 15 * len(TASKS) + 36 + 32


def per_device(tokens, w_in, w_out, cotangent):
    def turned(a):
        return a.reshape(2, 256, 192).transpose(0, 2, 1)

    vmem, far = pl.BlockSpec(memory_space=pltpu.VMEM), pl.BlockSpec(memory_space=pl.ANY)
    copies = copies_in_all()
    mixed, d_tokens, grad_in, grad_out = pl.pallas_call(
        kernel,
        out_shape=(
            jax.ShapeDtypeStruct((2, 192, 256), BF),
            jax.ShapeDtypeStruct((2, 192, 256), BF),
            jax.ShapeDtypeStruct((768, 384), BF),
            jax.ShapeDtypeStruct((384, 768), BF),
        ),
        in_specs=[vmem, vmem, far, far],
        out_specs=[vmem] * 4,
        scratch_shapes=[
            pltpu.VMEM((2, 2, 768, 512), BF),
            pltpu.VMEM((3, 768, 512), BF),
            pltpu.VMEM((3, 512, 768), BF),
            pltpu.SemaphoreType.DMA((2, 3, 4)),
            pltpu.VMEM((2, 2, 3, 256, 512), BF),
            pltpu.VMEM((2, 2, 3, 256, 512), BF),
            pltpu.VMEM((2, 3, 256, 512), F32),
            pltpu.VMEM((2, 2, 3, 3, 2, 32, 512), BF),
            pltpu.VMEM((2, 2, 3, 3, 2, 32, 512), BF),
            pltpu.VMEM((2, 3, 64, 512), F32),
            pltpu.VMEM((2, 2, 3, 512, 512), BF),
            pltpu.VMEM((6, 3, 2, 64, 768), BF),
            pltpu.VMEM((6, 3, 2, 64, 768), BF),
            pltpu.VMEM((6, 128, 768), F32),
            pltpu.VMEM((2, 2, 768, 512), F32),
            pltpu.VMEM((2, 2, 2, 4, 192, 256), BF),
            pltpu.VMEM((2, 2, 2, 4, 192, 256), BF),
            pltpu.SemaphoreType.DMA((copies,)),
            pltpu.SemaphoreType.DMA((copies,)),
        ],
        compiler_params=pltpu.CompilerParams(
            collective_id=0, has_side_effects=True, vmem_limit_bytes=62 * 2**20
        ),
        cost_estimate=pl.CostEstimate(flops=14_500_000_000, bytes_accessed=12_000_000, transcendentals=400_000),
    )(turned(tokens), turned(cotangent), w_in, w_out)

    def back(a):
        return a.transpose(0, 2, 1).reshape(512, 192)

    return (back(mixed), back(d_tokens), grad_in, grad_out)


def solution(mesh):
    split = Mesh(mesh.devices.reshape(2, 4, 4, 4, 2), ("zh", "x", "zl", "y", "c"))
    rows = P(("zh", "x"), ("y", "c", "zl"))
    return jax.shard_map(
        per_device,
        mesh=split,
        in_specs=(rows, P(("y", "c"), "zl"), P("zl", ("y", "c")), rows),
        out_specs=(rows, rows, P(("y", "c"), ("zl", "zh", "x")), P(("zl", "zh", "x"), ("y", "c"))),
        check_vma=False,
    )
```

time: 696 us -> 147 us (0.21)
  waiting for transfers between devices: 589 us -> 0 us
  Pallas kernels: 0 us -> 137 us
  matrix products: 44.5 us -> 0 us
  blocking collectives: 35.8 us -> 0 us
  between operations: 14.1 us -> 0.64 us
  other arithmetic: 9.49 us -> 0 us
    reduce_scatter x6 -> x0, waiting for transfers between devices: 532 us -> none  [the longest x1 203 us: per_device(): lax.psum_scatter(local_in, 'dp', scatter_dimension=1, tiled=True)]
    pallas_call x0 -> x1, Pallas kernels: none -> 137 us  [per_device(): pl.pallas_call(kernel, out_shape=(jax.ShapeDtypeStruct((2, 192, 256), BF)...]
    all_gather x2 -> x0, waiting for transfers between devices: 55.9 us -> none  [the longest x1 30.5 us: per_device(): hidden_all = lax.all_gather(hidden, 'my', axis=1, tiled=True)]
    dot_general x6 -> x0, matrix products: 44.5 us -> none  [the longest x2 16.4 us: rows_product(): lax.dot_general(left, right, (((0,), (0,)), ((), ())), preferred_element_...]
    all_gather x2 -> x0, blocking collectives: 35.8 us -> none  [the longest x1 19.3 us: per_device(): cot_all = lax.all_gather(cotangent, 'mx', axis=1, tiled=True)]
    convert_element_type x5 -> x0, other arithmetic: 9.49 us -> none  [the longest x1 2.62 us: per_device(): grad_pre = (d_hidden * derivative).astype(jnp.bfloat16)]
  transfers between devices with their start and end apart: 8 -> 0, of which waited for: 8 -> 0; matrix products, arithmetic and copies ran while one was open for 6% -> 0% of each run, Pallas kernels for 0% -> 0%
where the time goes in v1:
time: 147 us; the launch traced here: 146 us
  Pallas kernels  137 us (93%)
  local copies, waits for them, and re-layouts  8.87 us (6%)
    pallas_call x1, Pallas kernels, per_device(): pl.pallas_call(kernel, out_shape=(jax.ShapeDtypeStruct((2, 192, 256), BF)...  137 us
    unnamed x2, local copies, waits for them, and re-layouts  3.85 us
    reshape x2, local copies, waits for them, and re-layouts, back(): return a.transpose(0, 2, 1).reshape(512, 192)  3.23 us

profile of v1, /device:TPU:1, one launch (start us, length us, event | category | flops | bytes accessed | tf_op | source)
XLA Modules:
  0.0 146.3 jit_solution(17254059621706553121)
XLA Ops:
  0.6 1.8 %bitcast_bitcast_fusion = (bf16[2,192,256]{2,1,0:T(8,128)(2,1)}, bf16[2,192,256]{2,1,0:T(8,128)(2,1)}) fusion(bf16[24,2,8,256]{3,2,1,0:T(8,128)(2,1)} %bitcast.20, bf16[24,2,8,256]{3,2,1,0:T(8,128)(2,1)} %bitcast.21), kind=kLoop, calls=%fused_computation | loop fusion | bytes 786432 | tf_op jit(solution)/shard_map/transpose | solution.py:380
  2.4 136.8 %shard_map.75 = (bf16[2,192,256]{2,1,0:T(8,128)(2,1)}, bf16[2,192,256]{2,1,0:T(8,128)(2,1)}, bf16[768,384]{1,0:T(8,128)(2,1)}, bf16[384,768]{1,0:T(8,128)(2,1)}) custom-call(bf16[2,192,256]{2,1,0:T(8,128)(2,1)} %get-tuple-element.13.tok_in, bf16[2,192,256]{2,1,0:T(8,128)(2,1)} %get-tuple-element.12.cot_in, bf16[768,3072]{1,0:T(8,128)(2,1)} %w_in_hbm.1, ...), custom_call_target="tpu_custom_call" | custom-call | flops 14499999744 | bytes 12000000 | tf_op jit(solution)/shard_map/pallas_call | solution.py:384
  139.2 1.6 %copy.14 = bf16[2,24,8,256]{3,2,0,1:T(8,128)(2,1)} copy(bf16[2,24,8,256]{3,2,1,0:T(8,128)(2,1)} %bitcast.19) | data formatting | bytes 393216 | tf_op jit(solution)/shard_map/reshape | solution.py:422
  140.8 1.6 %copy.15 = bf16[2,24,8,256]{3,2,0,1:T(8,128)(2,1)} copy(bf16[2,24,8,256]{3,2,1,0:T(8,128)(2,1)} %bitcast.18) | data formatting | bytes 393216 | tf_op jit(solution)/shard_map/reshape | solution.py:422
  142.4 1.9 %copy.20 = bf16[768,384]{1,0:T(8,128)(2,1)} copy(bf16[768,384]{1,0:T(8,128)(2,1)} %get-tuple-element.20) | data formatting | bytes 1179648
  144.4 1.9 %copy.21 = bf16[384,768]{1,0:T(8,128)(2,1)} copy(bf16[384,768]{1,0:T(8,128)(2,1)} %get-tuple-element.21) | data formatting | bytes 1179648

commit v2 on v1

--- a/solution.py
+++ b/solution.py
@@ -18,8 +18,119 @@
     (1, 1, 1, 1),
     (1, 1, 2, 1),
 )
-LINKS = {"y+": (0.0244, 2.4), "y-": (0.0244, 2.4), "x+": (0.0244, 2.4), "x-": (0.0244, 2.4)}
-LINKS.update({"z+": (0.0244, 2.4), "z-": (0.0244, 2.4), "c": (0.0037, 0.9)})
+ORDER = (
+    ("g", 0, 0, 0),
+    ("g", 0, 1, 0),
+    ("g", 0, 0, 1),
+    ("g", 0, 1, 1),
+    ("g", 0, 0, 2),
+    "weights",
+    ("g", 0, 1, 2),
+    ("g", 0, 0, 3),
+    ("g", 1, 0, 0),
+    ("g", 0, 1, 3),
+    ("g", 1, 1, 0),
+    ("act", 0, 0),
+    ("h", 0, "other"),
+    ("h", 0, "own"),
+    ("g", 1, 0, 1),
+    ("act", 0, 1),
+    ("h", 1, "other"),
+    ("h", 0, "first"),
+    ("g", 1, 1, 1),
+    ("h", 1, "own"),
+    ("g", 1, 0, 2),
+    ("h", 1, "first"),
+    ("h", 0, "relay"),
+    ("g", 1, 1, 2),
+    ("h", 1, "relay"),
+    ("g", 1, 0, 3),
+    ("g", 1, 1, 3),
+    ("h", 0, "act"),
+    ("act", 1, 1),
+    ("h", 5, "other"),
+    ("h", 4, "other"),
+    ("act", 1, 0),
+    ("h", 3, "other"),
+    ("h", 1, "act"),
+    ("h", 3, "own"),
+    ("h", 2, "other"),
+    ("h", 0, "pass"),
+    ("h", 3, "first"),
+    ("h", 4, "own"),
+    ("h", 1, "pass"),
+    ("h", 2, "own"),
+    ("h", 2, "first"),
+    ("h", 0, "last"),
+    ("h", 0, "done"),
+    ("h", 3, "relay"),
+    ("z", 0, 0, "mul"),
+    ("z", 0, 0, 0),
+    ("h", 1, "last"),
+    ("h", 5, "own"),
+    ("h", 2, "relay"),
+    ("h", 1, "done"),
+    ("w", 0, 0, "mul"),
+    ("z", 0, 0, 1),
+    ("h", 4, "first"),
+    ("h", 5, "first"),
+    ("z", 0, 1, "mul"),
+    ("z", 0, 1, 0),
+    ("w", 0, 2, "mul"),
+    ("h", 2, "act"),
+    ("z", 0, 1, 1),
+    ("w", 0, 0, "relay"),
+    ("h", 3, "act"),
+    ("w", 0, 1, "mul"),
+    ("z", 0, 0, 2),
+    ("w", 0, 2, "relay"),
+    ("h", 5, "relay"),
+    ("h", 4, "relay"),
+    ("z", 0, 1, 2),
+    ("h", 2, "pass"),
+    ("z", 0, 0, 3),
+    ("h", 3, "pass"),
+    ("h", 5, "act"),
+    ("w", 0, 0, "end"),
+    ("h", 4, "act"),
+    ("h", 2, "last"),
+    ("h", 3, "last"),
+    ("z", 0, 1, 3),
+    ("w", 0, 1, "relay"),
+    ("h", 5, "pass"),
+    ("h", 3, "done"),
+    ("h", 2, "done"),
+    ("w", 1, 0, "mul"),
+    ("h", 4, "pass"),
+    ("z", 1, 0, "mul"),
+    ("h", 5, "last"),
+    ("z", 0, 0, "end"),
+    ("h", 5, "done"),
+    ("z", 0, 1, "end"),
+    ("z", 1, 0, 0),
+    ("h", 4, "last"),
+    ("w", 1, 2, "mul"),
+    ("h", 4, "done"),
+    ("z", 1, 1, "mul"),
+    ("z", 1, 1, 0),
+    ("z", 1, 0, 1),
+    ("w", 1, 1, "mul"),
+    ("w", 0, 1, "end"),
+    ("w", 0, 2, "end"),
+    ("w", 1, 2, "relay"),
+    ("z", 1, 1, 1),
+    ("z", 1, 0, 2),
+    ("w", 1, 0, "relay"),
+    ("z", 1, 1, 2),
+    ("w", 1, 1, "relay"),
+    ("z", 1, 0, 3),
+    ("w", 1, 2, "end"),
+    ("z", 1, 1, 3),
+    ("z", 1, 0, "end"),
+    ("w", 1, 1, "end"),
+    ("w", 1, 0, "end"),
+    ("z", 1, 1, "end"),
+)
 
 
 def gelu_parts(pre_act):
@@ -45,52 +156,9 @@
     def step(self, name, needs, cost, body, sends=()):
         self.steps[name] = (tuple(needs), cost, body, tuple(sends))
 
-    def order(self):
-        started_by = {c: s for s, v in self.steps.items() for c in v[3]}
-        users = {s: [] for s in self.steps}
-        for s, (needs, _, _, _) in self.steps.items():
-            for n in needs:
-                if n in self.copies:
-                    link, kb = self.copies[n][:2]
-                    per_kb, latency = LINKS[link]
-                    users[started_by[n]].append((s, latency + per_kb * kb))
-                else:
-                    users[n].append((s, 0.0))
-        level = {}
-
-        def height(s):
-            if s not in level:
-                level[s] = self.steps[s][1] + max([height(u) + d for u, d in users[s]], default=0.0)
-            return level[s]
-
-        now, done, free = 0.0, {}, {}
-        todo, result = list(self.steps), []
-        while todo:
-            best = None
-            for s in todo:
-                if any(n not in done for n in self.steps[s][0]):
-                    continue
-                at = max([done[n] for n in self.steps[s][0]], default=0.0)
-                key = (max(at, now), -height(s))
-                if best is None or key < best[0]:
-                    best = (key, s)
-            (at, _), s = best
-            now = at + self.steps[s][1]
-            done[s] = now
-            for c in self.steps[s][3]:
-                now += 0.05
-                link, kb = self.copies[c][:2]
-                per_kb, latency = LINKS[link]
-                free[link] = max(free.get(link, 0.0), now) + per_kb * kb
-                done[c] = free[link] + latency
-            todo.remove(s)
-            result.append(s)
-        self.estimate = now
-        return result
-
 
 def kernel(tok_in, cot_in, w_in_hbm, w_out_hbm, mix_out, dtok_out, gin_out, gout_out, *scratch):
-    (act, w_in, w_out, w_sem, csnd, crcv, own, ysnd, yrcv, deriv, hid, xsnd, xrcv, xown, zacc, zsnd, zrcv, send_sem, recv_sem) = scratch
+    (act, w_in, w_out, w_sem, csnd, crcv, own, ysnd, yrcv, deriv, hid, xsnd, xrcv, xown, xtmp, zacc, zsnd, zrcv, send_sem, recv_sem) = scratch
     zh, x, zl = lax.axis_index("zh"), lax.axis_index("x"), lax.axis_index("zl")
     y, c = lax.axis_index("y"), lax.axis_index("c")
     z = zh * 4 + zl
@@ -129,7 +197,7 @@
         source = (tok_in, cot_in)[a]
 
         def begin():
-            place(a, h, z)[...] = source[h]
+            place(a, h, z)[...] = source[:, pl.ds(h * 256, 256)]
 
         for s in range(4):
             for sign, d in ((1, "z+"), (-1, "z-")):
@@ -159,26 +227,16 @@
 
         def product(j, row):
             if p == 0:
-                return dot(w_in[j, :, pl.ds(row, 128)], act[0, h], (0, 0))
-            return dot(w_out[j, pl.ds(row, 128), :], act[1, h], (1, 0))
+                return dot(w_in[j, :, pl.ds(row, 256)], act[0, h], (0, 0))
+            return dot(w_out[j, pl.ds(row, 256), :], act[1, h], (1, 0))
 
         def other_half():
-            def body(i, _):
-                j, k = j0 + i // 2, lax.rem(i, 2)
-                row = pl.multiple_of((1 - c) * 256 + k * 128, 128)
-                csnd[p, h, j, pl.ds(pl.multiple_of(k * 128, 128), 128), :] = product(j, row).astype(BF)
-                return 0
-
-            lax.fori_loop(0, 2 * nj, body, 0)
+            for j in js:
+                csnd[p, h, j] = product(j, pl.multiple_of((1 - c) * 256, 256)).astype(BF)
 
         def own_half():
-            def body(i, _):
-                j, k = j0 + i // 2, lax.rem(i, 2)
-                row = pl.multiple_of(c * 256 + k * 128, 128)
-                own[h, j, pl.ds(pl.multiple_of(k * 128, 128), 128), :] = product(j, row)
-                return 0
-
-            lax.fori_loop(0, 2 * nj, body, 0)
+            for j in js:
+                own[h, j] = product(j, pl.multiple_of(c * 256, 256))
 
         def mine(j, rel, half):
             row = pl.ds(pl.multiple_of(lax.rem(y + rel, 4) * 64 + half * 32, 32), 32)
@@ -218,17 +276,17 @@
             src, dst = ysnd.at[p, h, cut, rel - 1, half], yrcv.at[p, h, cut, rel - 1, half]
             plan.copy(n("r", rel, half), d, 32 * nj, src, dst, dst)
         needs = [("act", p, h), "weights"] + ([n0 for n0 in fwd_done if p == 1])
-        plan.step(n("other"), needs, 0.25 * nj, other_half, [n("c")])
-        plan.step(n("own"), [n("other")], 0.25 * nj, own_half)
-        plan.step(n("first"), [n("own"), n("c")], 0.15 * nj, first_sums, [n("r", 2, 0), n("r", 2, 1), n("r", 1, 1), n("r", 3, 0)])
-        plan.step(n("relay"), [n("first"), n("r", 2, 0), n("r", 2, 1)], 0.1 * nj, relay_sums, [n("r", 1, 0), n("r", 3, 1)])
+        plan.step(n("other"), needs, 0.4 * nj, other_half, [n("c")])
+        plan.step(n("own"), [n("other")], 0.4 * nj, own_half)
+        plan.step(n("first"), [n("own"), n("c")], 0.1 * nj, first_sums, [n("r", 2, 0), n("r", 2, 1), n("r", 1, 1), n("r", 3, 0)])
+        plan.step(n("relay"), [n("first"), n("r", 2, 0), n("r", 2, 1)], 0.06 * nj, relay_sums, [n("r", 1, 0), n("r", 3, 1)])
         plan.copy(n("a", "+"), "y+", 64 * nj, piece(c, 0), piece(c, 0), piece(c, 3))
         plan.copy(n("a", "-"), "y-", 64 * nj, piece(c, 0), piece(c, 0), piece(c, 1))
         plan.copy(n("f", "+"), "y+", 32 * nj, piece(c, 3, 0, 32), piece(c, 3, 0, 32), piece(c, 2, 0, 32))
         plan.copy(n("f", "-"), "y-", 32 * nj, piece(c, 1, 32, 32), piece(c, 1, 32, 32), piece(c, 2, 32, 32))
         for rel in range(4):
             plan.copy(n("k", rel), "c", 64 * nj, piece(c, rel), piece(c, rel), piece(1 - c, rel))
-        plan.step(n("act"), [n("relay")] + [n("r", *k) for k in ((1, 1), (3, 0), (1, 0), (3, 1))], 0.2 * nj, activate, [n("a", "+"), n("a", "-"), n("k", 0)])
+        plan.step(n("act"), [n("relay")] + [n("r", *k) for k in ((1, 1), (3, 0), (1, 0), (3, 1))], 0.12 * nj, activate, [n("a", "+"), n("a", "-"), n("k", 0)])
         plan.step(n("pass"), [n("a", "+"), n("a", "-")], 0.05, None, [n("f", "+"), n("f", "-"), n("k", 1), n("k", 3)])
         plan.step(n("last"), [n("f", "+"), n("f", "-")], 0.05, None, [n("k", 2)])
         plan.step(n("done"), [n("k", rel) for rel in range(4)], 0.0, None)
@@ -246,26 +304,18 @@
         other = 1 - p
         slot = p * 3 + j
 
-        def product(rel):
-            row = pl.ds(pl.multiple_of(lax.rem(x + rel, 4) * 128, 128), 128)
-            return sum(dot(hid[p, h, j, row, :], act[other, h], (1, 1)) for h in range(2))
-
         def multiply():
-            def body(i, _):
-                total = product(3 - i).astype(BF)
-                xsnd[slot, 2 - i, 0] = total[:64]
-                xsnd[slot, 2 - i, 1] = total[64:]
-                return 0
-
-            lax.fori_loop(0, 3, body, 0)
-
-        def multiply_own():
-            xown[slot] = product(0)
+            xtmp[...] = sum(dot(hid[p, h, j], act[other, h], (1, 1)) for h in range(2))
+            for to in range(4):
+                for half in range(2):
+                    xsnd[slot, to, half] = xtmp[pl.ds(to * 128 + half * 64, 64), :].astype(BF)
+            xown[slot] = xtmp[pl.ds(pl.multiple_of(x * 128, 128), 128), :]
 
         def relay_sums():
             for rel, half in ((1, 0), (3, 1)):
-                total = xsnd[slot, rel - 1, half].astype(F32) + xrcv[slot, 1, half].astype(F32)
-                xsnd[slot, rel - 1, half] = total.astype(BF)
+                to = lax.rem(x + rel, 4)
+                total = xsnd[slot, to, half].astype(F32) + xrcv[slot, 1, half].astype(F32)
+                xsnd[slot, to, half] = total.astype(BF)
 
         def finish():
             for half in range(2):
@@ -278,13 +328,12 @@
 
         n = lambda *rest: ("w", p, j) + rest
         for rel, half, d in ((2, 0, "x+"), (2, 1, "x-"), (1, 1, "x+"), (3, 0, "x-"), (1, 0, "x+"), (3, 1, "x-")):
-            plan.copy(n("r", rel, half), d, 96, xsnd.at[slot, rel - 1, half], xrcv.at[slot, rel - 1, half], xrcv.at[slot, rel - 1, half])
+            plan.copy(n("r", rel, half), d, 96, xsnd.at[slot, lax.rem(x + rel, 4), half], xrcv.at[slot, rel - 1, half], xrcv.at[slot, rel - 1, half])
         needs = [("act", other, h) for h in range(2)]
         needs += [("h", t, "done") for t, (q, h, j0, nj) in enumerate(TASKS) if q == p and j0 <= j < j0 + nj]
-        plan.step(n("mul"), needs, 0.9, multiply, [n("r", 2, 0), n("r", 2, 1), n("r", 1, 1), n("r", 3, 0)])
-        plan.step(n("own"), [n("mul")], 0.3, multiply_own)
+        plan.step(n("mul"), needs, 1.2, multiply, [n("r", 2, 0), n("r", 2, 1), n("r", 1, 1), n("r", 3, 0)])
         plan.step(n("relay"), [n("mul"), n("r", 2, 0), n("r", 2, 1)], 0.15, relay_sums, [n("r", 1, 0), n("r", 3, 1)])
-        plan.step(n("end"), [n("own")] + [n("r", *k) for k in ((1, 1), (3, 0), (1, 0), (3, 1))], 0.3, finish)
+        plan.step(n("end"), [n("r", *k) for k in ((1, 1), (3, 0), (1, 0), (3, 1))], 0.25, finish)
 
     for p in range(2):
         for j in range(3):
@@ -292,19 +341,10 @@
 
     def result(p, h):
         def multiply():
-            def body(i, _):
-                row = pl.ds(pl.multiple_of(i * 256, 256), 256)
-                total = None
-                for j in range(3):
-                    if p == 0:
-                        term = dot(w_out[j, :, row], hid[0, h, j], (0, 0))
-                    else:
-                        term = dot(w_in[j, row, :], hid[1, h, j], (1, 0))
-                    total = term if total is None else total + term
-                zacc[p, h, row, :] = total
-                return 0
-
-            lax.fori_loop(0, 3, body, 0)
+            if p == 0:
+                zacc[p, h] = sum(dot(w_out[j], hid[0, h, j], (0, 0)) for j in range(3))
+            else:
+                zacc[p, h] = sum(dot(w_in[j], hid[1, h, j], (1, 0)) for j in range(3))
 
         def mine(rel, first=0, rows=192):
             at = lax.rem(z + rel, 8)
@@ -329,7 +369,7 @@
 
         def finish():
             total = mine(0) + zrcv[p, h, 0, 3].astype(F32) + zrcv[p, h, 1, 3].astype(F32)
-            (mix_out, dtok_out)[p][h] = total.astype(BF)
+            (mix_out, dtok_out)[p][:, pl.ds(h * 256, 256)] = total.astype(BF)
 
         n = lambda *rest: ("z", p, h) + rest
         for d, link in ((0, "z+"), (1, "z-")):
@@ -337,11 +377,11 @@
                 rows = pl.ds(0, 192) if s else pl.ds(d * 96, 96)
                 plan.copy(n("r", s, d), link, 96 if s else 48, zsnd.at[p, h, d, s, rows], zrcv.at[p, h, d, s, rows], zrcv.at[p, h, d, s, rows])
         needs = [("h", t, "done") for t, (q, hh, _, _) in enumerate(TASKS) if q == p and hh == h]
-        plan.step(n("mul"), needs, 1.2, multiply)
+        plan.step(n("mul"), needs, 1.45, multiply)
         plan.step(n(0), [n("mul")], 0.1, first, [n("r", 0, 0), n("r", 0, 1)])
         for s in range(1, 4):
-            plan.step(n(s), [n("r", s - 1, 0), n("r", s - 1, 1)], 0.3, add(s), [n("r", s, 0), n("r", s, 1)])
-        plan.step(n("end"), [n("r", 3, 0), n("r", 3, 1)], 0.2, finish)
+            plan.step(n(s), [n("r", s - 1, 0), n("r", s - 1, 1)], 0.15, add(s), [n("r", s, 0), n("r", s, 1)])
+        plan.step(n("end"), [n("r", 3, 0), n("r", 3, 1)], 0.15, finish)
 
     for p in range(2):
         for h in range(2):
@@ -356,7 +396,7 @@
         src, dst = (there, there) if landing else (src, dst)
         return pltpu.make_async_remote_copy(src, dst, send_sem.at[i], recv_sem.at[i], device_id=targets[link], device_id_type=MESH)
 
-    for name in plan.order():
+    for name in ORDER:
         needs, _, body, sends = plan.steps[name]
         for need in needs:
             if need in plan.copies and need not in waited:
@@ -367,6 +407,8 @@
         for copy in sends:
             remote(copy, False).start()
             sent.append(copy)
+        while len(sent) > 40:
+            remote(sent.pop(0), False).wait_send()
     for copy in sent:
         remote(copy, False).wait_send()
 
@@ -375,20 +417,18 @@
     return 32 + 15 * len(TASKS) + 36 + 32
 
 
+def hand_over(*refs):
+    for i in range(4):
+        refs[4 + i][...] = refs[i][...]
+
+
 def per_device(tokens, w_in, w_out, cotangent):
-    def turned(a):
-        return a.reshape(2, 256, 192).transpose(0, 2, 1)
-
     vmem, far = pl.BlockSpec(memory_space=pltpu.VMEM), pl.BlockSpec(memory_space=pl.ANY)
     copies = copies_in_all()
-    mixed, d_tokens, grad_in, grad_out = pl.pallas_call(
+    shapes = [jax.ShapeDtypeStruct(s, BF) for s in ((192, 512), (192, 512), (768, 384), (384, 768))]
+    results = pl.pallas_call(
         kernel,
-        out_shape=(
-            jax.ShapeDtypeStruct((2, 192, 256), BF),
-            jax.ShapeDtypeStruct((2, 192, 256), BF),
-            jax.ShapeDtypeStruct((768, 384), BF),
-            jax.ShapeDtypeStruct((384, 768), BF),
-        ),
+        out_shape=shapes,
         in_specs=[vmem, vmem, far, far],
         out_specs=[vmem] * 4,
         scratch_shapes=[
@@ -403,9 +443,10 @@
             pltpu.VMEM((2, 2, 3, 3, 2, 32, 512), BF),
             pltpu.VMEM((2, 3, 64, 512), F32),
             pltpu.VMEM((2, 2, 3, 512, 512), BF),
-            pltpu.VMEM((6, 3, 2, 64, 768), BF),
+            pltpu.VMEM((6, 4, 2, 64, 768), BF),
             pltpu.VMEM((6, 3, 2, 64, 768), BF),
             pltpu.VMEM((6, 128, 768), F32),
+            pltpu.VMEM((512, 768), F32),
             pltpu.VMEM((2, 2, 768, 512), F32),
             pltpu.VMEM((2, 2, 2, 4, 192, 256), BF),
             pltpu.VMEM((2, 2, 2, 4, 192, 256), BF),
@@ -416,12 +457,15 @@
             collective_id=0, has_side_effects=True, vmem_limit_bytes=62 * 2**20
         ),
         cost_estimate=pl.CostEstimate(flops=14_500_000_000, bytes_accessed=12_000_000, transcendentals=400_000),
-    )(turned(tokens), turned(cotangent), w_in, w_out)
-
-    def back(a):
-        return a.transpose(0, 2, 1).reshape(512, 192)
-
-    return (back(mixed), back(d_tokens), grad_in, grad_out)
+    )(tokens.T, cotangent.T, w_in, w_out)
+
+    mixed, d_tokens, grad_in, grad_out = pl.pallas_call(
+        hand_over,
+        out_shape=shapes,
+        in_specs=[vmem] * 4,
+        out_specs=[vmem] * 4,
+    )(*results)
+    return (mixed.T, d_tokens.T, grad_in, grad_out)
 
 
 def solution(mesh):

time: 147 us -> 118 us (0.80)
  Pallas kernels: 137 us -> 117 us
  local copies, waits for them, and re-layouts: 8.87 us -> 0 us
    pallas_call x1 -> x2, Pallas kernels: 137 us -> 117 us  [the longest x1 114 us: per_device(): pl.pallas_call(kernel, out_shape=shapes, in_specs=[vmem, vmem, far, far],...]
    unnamed x2 -> x0, local copies, waits for them, and re-layouts: 3.85 us -> none
    reshape x2 -> x0, local copies, waits for them, and re-layouts: 3.23 us -> none  [back(): return a.transpose(0, 2, 1).reshape(512, 192)]
    transpose x1 -> x0, local copies, waits for them, and re-layouts: 1.79 us -> none  [turned(): return a.reshape(2, 256, 192).transpose(0, 2, 1)]
where the time goes in v2:
time: 118 us; the launch traced here: 117 us
  Pallas kernels  117 us (99%)
    pallas_call x1, Pallas kernels, per_device(): pl.pallas_call(kernel, out_shape=shapes, in_specs=[vmem, vmem, far, far],...  114 us
    pallas_call x1, Pallas kernels, per_device(): pl.pallas_call(hand_over, out_shape=shapes, in_specs=[vmem] * 4, out_spec...  2.6 us

profile of v2, /device:TPU:1, one launch (start us, length us, event | category | flops | bytes accessed | tf_op | source)
XLA Modules:
  0.0 117.5 jit_solution(310855951557298761)
XLA Ops:
  0.6 114.2 %shard_map.75 = (bf16[192,512]{1,0:T(8,128)(2,1)}, bf16[192,512]{1,0:T(8,128)(2,1)}, bf16[768,384]{1,0:T(8,128)(2,1)}, bf16[384,768]{1,0:T(8,128)(2,1)}) custom-call(bf16[192,512]{1,0:T(8,128)(2,1)} %bitcast.4, bf16[192,512]{1,0:T(8,128)(2,1)} %bitcast.5, bf16[768,3072]{1,0:T(8,128)(2,1)} %w_in_hbm.1, bf16[3072,768]{1,0:T(8,128)(2,1)} %w_out_hbm.1), custom_call_target="tpu_custom_call" | custom-call | flops 14499999744 | bytes 12000000 | tf_op jit(solution)/shard_map/pallas_call | solution.py:429
  114.9 2.6 %shard_map.76 = (bf16[192,512]{1,0:T(8,128)(2,1)}, bf16[192,512]{1,0:T(8,128)(2,1)}, bf16[768,384]{1,0:T(8,128)(2,1)}, bf16[384,768]{1,0:T(8,128)(2,1)}) custom-call(bf16[192,512]{1,0:T(8,128)(2,1)} %get-tuple-element.12.refs_0_, bf16[192,512]{1,0:T(8,128)(2,1)} %get-tuple-element.13.refs_1_, bf16[768,384]{1,0:T(8,128)(2,1)} %get-tuple-element.14.refs_2_, ...), custom_call_target="tpu_custom_call" | custom-call | tf_op jit(solution)/shard_map/pallas_call | solution.py:462

commit v3 on v2

v3 whole, which is shorter than its diff:
```python
import jax
import jax.numpy as jnp
from jax import lax
from jax.experimental import pallas as pl
from jax.experimental.pallas import tpu as pltpu
from jax.sharding import Mesh
from jax.sharding import PartitionSpec as P

MESH = pl.DeviceIdType.MESH
BF = jnp.bfloat16
F32 = jnp.float32

TASKS = (
    (0, 0, 1, 0, 1),
    (0, 0, 1, 1, 1),
    (0, 0, 1, 2, 1),
    (0, 1, 1, 0, 1),
    (0, 1, 1, 1, 1),
    (0, 1, 1, 2, 1),
    (0, 2, 2, 0, 1),
    (0, 2, 2, 1, 1),
    (0, 2, 2, 2, 1),
    (1, 0, 2, 0, 1),
    (1, 2, 2, 0, 1),
    (1, 0, 2, 1, 1),
    (1, 2, 2, 1, 1),
    (1, 0, 2, 2, 1),
    (1, 2, 2, 2, 1),
)
SUMS = (((0, 2), (2, 2)), ((0, 1), (1, 1), (2, 1), (3, 1)))
FAR_GATHERS = ((0, 0),)
FAR_SUMS = ()
FAR_HIDDEN = ()
ORDER = (
    ("g", 0, 1, 0),
    ("g", 0, 0, 0),
    ("g", 0, 3, 0),
    ("g", 0, 1, 1),
    ("g", 0, 2, 0),
    ("g", 0, 0, 1),
    ("g", 0, 1, 2),
    ("g", 0, 2, 1),
    ("g", 0, 3, 1),
    "weights",
    ("act", 0, 0),
    ("h", 2, "other"),
    ("h", 0, "other"),
    ("h", 1, "other"),
    ("g", 0, 1, 3),
    ("h", 1, "own"),
    ("g", 1, 2, 0),
    ("h", 2, "own"),
    ("h", 2, "first"),
    ("h", 0, "own"),
    ("g", 0, 2, 2),
    ("h", 0, "first"),
    ("g", 0, 3, 2),
    ("g", 1, 3, 0),
    ("h", 1, "first"),
    ("act", 0, 1),
    ("h", 5, "other"),
    ("h", 3, "other"),
    ("h", 2, "relay"),
    ("h", 5, "own"),
    ("g", 1, 0, 0),
    ("h", 4, "other"),
    ("h", 0, "relay"),
    ("h", 5, "first"),
    ("h", 4, "own"),
    ("h", 3, "own"),
    ("h", 1, "relay"),
    ("g", 0, 2, 3),
    ("h", 3, "first"),
    ("g", 0, 3, 3),
    ("g", 1, 2, 1),
    ("h", 4, "first"),
    ("h", 2, "act"),
    ("g", 1, 3, 1),
    ("h", 5, "relay"),
    ("h", 0, "act"),
    ("g", 1, 1, 0),
    ("g", 1, 0, 1),
    ("h", 1, "act"),
    ("act", 0, 2),
    ("h", 3, "relay"),
    ("act", 0, 3),
    ("h", 8, "other"),
    ("h", 4, "relay"),
    ("h", 6, "other"),
    ("h", 8, "own"),
    ("h", 2, "pass"),
    ("h", 5, "act"),
    ("g", 1, 2, 2),
    ("h", 8, "first"),
    ("g", 1, 3, 2),
    ("h", 6, "own"),
    ("h", 7, "other"),
    ("h", 6, "first"),
    ("g", 1, 1, 1),
    ("g", 1, 0, 2),
    ("h", 2, "last"),
    ("h", 3, "act"),
    ("h", 7, "own"),
    ("h", 7, "first"),
    ("g", 1, 2, 3),
    ("h", 8, "relay"),
    ("h", 0, "pass"),
    ("g", 1, 3, 3),
    ("h", 6, "relay"),
    ("h", 5, "pass"),
    ("g", 1, 1, 2),
    ("h", 1, "pass"),
    ("h", 7, "relay"),
    ("g", 1, 0, 3),
    ("act", 1, 2),
    ("h", 4, "act"),
    ("act", 1, 3),
    ("h", 10, "other"),
    ("h", 8, "act"),
    ("h", 3, "pass"),
    ("h", 0, "last"),
    ("h", 6, "act"),
    ("g", 1, 1, 3),
    ("h", 14, "other"),
    ("h", 14, "own"),
    ("h", 7, "act"),
    ("h", 5, "last"),
    ("h", 1, "last"),
    ("act", 1, 0),
    ("h", 4, "pass"),
    ("h", 2, "done"),
    ("h", 10, "own"),
    ("h", 14, "first"),
    ("h", 12, "other"),
    ("h", 8, "pass"),
    ("act", 1, 1),
    ("h", 11, "other"),
    ("h", 13, "other"),
    ("h", 5, "done"),
    ("h", 6, "pass"),
    ("h", 9, "other"),
    ("h", 11, "own"),
    ("h", 7, "pass"),
    ("h", 10, "first"),
    ("h", 13, "own"),
    ("h", 14, "relay"),
    ("h", 13, "first"),
    ("h", 12, "own"),
    ("h", 9, "own"),
    ("h", 12, "first"),
    ("h", 0, "done"),
    ("h", 8, "last"),
    ("h", 6, "last"),
    ("h", 3, "last"),
    ("h", 7, "last"),
    ("h", 9, "first"),
    ("h", 8, "done"),
    ("h", 4, "last"),
    ("w", 0, 2, "mul"),
    ("h", 4, "done"),
    ("h", 10, "relay"),
    ("h", 7, "done"),
    ("h", 6, "done"),
    ("z", 0, 2, "mul"),
    ("z", 0, 2, 0),
    ("h", 13, "relay"),
    ("h", 3, "done"),
    ("h", 11, "first"),
    ("h", 12, "relay"),
    ("h", 14, "act"),
    ("h", 1, "done"),
    ("z", 0, 0, "mul"),
    ("z", 0, 0, 0),
    ("w", 0, 1, "mul"),
    ("z", 0, 2, 1),
    ("h", 13, "act"),
    ("h", 9, "relay"),
    ("h", 10, "act"),
    ("w", 0, 0, "mul"),
    ("h", 11, "relay"),
    ("z", 0, 0, 1),
    ("h", 14, "pass"),
    ("h", 12, "act"),
    ("w", 0, 1, "relay"),
    ("h", 13, "pass"),
    ("z", 0, 2, 2),
    ("w", 0, 2, "relay"),
    ("h", 9, "act"),
    ("h", 11, "act"),
    ("h", 10, "pass"),
    ("z", 0, 0, 2),
    ("h", 13, "last"),
    ("h", 12, "pass"),
    ("h", 14, "last"),
    ("w", 0, 0, "relay"),
    ("z", 0, 2, 3),
    ("h", 9, "pass"),
    ("h", 13, "done"),
    ("h", 14, "done"),
    ("w", 1, 2, "mul"),
    ("h", 11, "pass"),
    ("h", 10, "last"),
    ("z", 0, 0, 3),
    ("h", 12, "last"),
    ("h", 9, "last"),
    ("h", 10, "done"),
    ("h", 12, "done"),
    ("z", 1, 3, "mul"),
    ("z", 1, 2, "mul"),
    ("z", 1, 2, 0),
    ("z", 1, 3, 0),
    ("h", 11, "last"),
    ("h", 9, "done"),
    ("w", 1, 0, "mul"),
    ("h", 11, "done"),
    ("z", 1, 1, "mul"),
    ("z", 1, 1, 0),
    ("z", 1, 0, "mul"),
    ("z", 1, 0, 0),
    ("w", 1, 2, "relay"),
    ("z", 1, 2, 1),
    ("w", 0, 0, "end"),
    ("z", 1, 3, 1),
    ("w", 0, 2, "end"),
    ("w", 1, 1, "mul"),
    ("z", 1, 1, 1),
    ("z", 1, 0, 1),
    ("z", 0, 0, "end"),
    ("w", 0, 1, "end"),
    ("z", 1, 2, 2),
    ("z", 1, 3, 2),
    ("z", 1, 1, 2),
    ("z", 1, 0, 2),
    ("w", 1, 0, "relay"),
    ("z", 1, 2, 3),
    ("z", 1, 3, 3),
    ("z", 0, 2, "end"),
    ("w", 1, 1, "relay"),
    ("z", 1, 1, 3),
    ("z", 1, 0, 3),
    ("z", 1, 2, "end"),
    ("z", 1, 3, "end"),
    ("z", 1, 1, "end"),
    ("w", 1, 0, "end"),
    ("w", 1, 2, "end"),
    ("w", 1, 1, "end"),
    ("z", 1, 0, "end"),
)


def gelu_parts(pre_act):
    root_half = 0.7071067811865476
    inv_root_two_pi = 0.3989422804014327
    cumul = 0.5 * (1.0 + lax.erf(pre_act * root_half))
    value = pre_act * cumul
    derivative = cumul + pre_act * jnp.exp(-0.5 * pre_act * pre_act) * inv_root_two_pi
    return (value, derivative)


def dot(left, right, dims):
    return lax.dot_general(left, right, ((dims[:1], dims[1:]), ((), ())), preferred_element_type=F32)


class Plan:
    def __init__(self):
        self.steps, self.copies = {}, {}

    def copy(self, name, link, src, dst, landing):
        self.copies[name] = (link, src, dst, landing)

    def step(self, name, needs, body, sends=()):
        self.steps[name] = (tuple(needs), body, tuple(sends))


def kernel(tok_in, cot_in, w_in_hbm, w_out_hbm, mix_out, dtok_out, gin_out, gout_out, *scratch):
    (act, w_in, w_out, w_sem, csnd, crcv, own, ysnd, yrcv, deriv, hid, xsnd, xrcv, xown, xtmp, zacc, zsnd, zrcv, send_sem, recv_sem) = scratch
    zh, x, zl = lax.axis_index("zh"), lax.axis_index("x"), lax.axis_index("zl")
    y, c = lax.axis_index("y"), lax.axis_index("c")
    z = zh * 4 + zl

    def along(axis, by):
        if axis == "z":
            to = lax.rem(z + by + 8, 8)
            return {"zh": to // 4, "zl": lax.rem(to, 4)}
        return {axis: lax.rem(lax.axis_index(axis) + by + 4, 4)}

    targets = {a + s: along(a, 1 if s == "+" else -1) for a in "xyz" for s in "+-"}
    targets["c"] = {"c": 1 - c}
    if FAR_GATHERS or FAR_SUMS:
        targets.update({"z++": along("z", 2), "z--": along("z", -2)})
    if FAR_HIDDEN:
        targets["y2"] = along("y", 2)

    plan = Plan()

    loads = []
    for j in range(3):
        for xx in range(4):
            at = pl.multiple_of(zh * 1536 + xx * 384 + j * 128, 128)
            part = pl.ds(xx * 128, 128)
            loads.append(pltpu.make_async_copy(w_in_hbm.at[:, pl.ds(at, 128)], w_in.at[j, :, part], w_sem.at[0, j, xx]))
            loads.append(pltpu.make_async_copy(w_out_hbm.at[pl.ds(at, 128), :], w_out.at[j, part, :], w_sem.at[1, j, xx]))
    for load in loads:
        load.start()
    barrier = pltpu.get_barrier_semaphore()
    for target in targets.values():
        pl.semaphore_signal(barrier, inc=1, device_id=target, device_id_type=MESH)
    pl.semaphore_wait(barrier, len(targets))

    def place(a, q, at, first=0, rows=192):
        at = lax.rem(at + 16, 8)
        row = pl.multiple_of(lax.rem(at, 4) * 192 + first, 32)
        return act.at[a, q, pl.ds(row, rows), pl.ds(pl.multiple_of((at // 4) * 128, 128), 128)]

    def gather(a, q):
        source = (tok_in, cot_in)[a]

        def begin():
            place(a, q, z)[...] = source[:, pl.ds(q * 128, 128)]

        n = lambda *rest: ("g", a, q) + rest
        if (a, q) in FAR_GATHERS:
            for sign, d in ((1, "z+"), (-1, "z-")):
                near, far, half = z - sign, z - 2 * sign, (0 if sign == 1 else 96, 96)
                plan.copy(n(0, d), d + d[1], place(a, q, z), place(a, q, z), place(a, q, far))
                plan.copy(n(1, d), d, place(a, q, z), place(a, q, z), place(a, q, near))
                plan.copy(n(2, d), d + d[1], place(a, q, far, *half), place(a, q, far, *half), place(a, q, z - 4 * sign, *half))
                plan.copy(n(3, d), d, place(a, q, far), place(a, q, far), place(a, q, z - 3 * sign))
            plan.step(n(0), [], begin, [n(s, d) for s in (0, 1) for d in ("z+", "z-")])
            plan.step(n(1), [n(0, d) for d in ("z+", "z-")], None, [n(s, d) for s in (2, 3) for d in ("z+", "z-")])
            plan.step(("act", a, q), [n(s, d) for s in (1, 2, 3) for d in ("z+", "z-")], None)
            return
        for s in range(4):
            for sign, d in ((1, "z+"), (-1, "z-")):
                first, rows = (0, 192) if s < 3 else ((0, 96) if sign == 1 else (96, 96))
                here = place(a, q, z - sign * s, first, rows)
                there = place(a, q, z - sign * (s + 1), first, rows)
                plan.copy(n(s, d), d, here, here, there)
            needs = [n(s - 1, d) for d in ("z+", "z-")] if s else []
            plan.step(n(s), needs, begin if s == 0 else None, [n(s, d) for d in ("z+", "z-")])
        plan.step(("act", a, q), [n(3, d) for d in ("z+", "z-")], None)

    for a in range(2):
        for q in range(4):
            gather(a, q)

    def wait_weights():
        for load in loads:
            load.wait()

    plan.step("weights", [], wait_weights)

    def hidden_task(t):
        p, q0, nq, j0, nj = TASKS[t]
        units = [(q, j) for q in range(q0, q0 + nq) for j in range(j0, j0 + nj)]
        cut = (p, pl.ds(q0, nq), pl.ds(j0, nj))

        def product(q, j, row):
            if p == 0:
                return dot(w_in[j, :, pl.ds(row, 256)], act[0, q], (0, 0))
            return dot(w_out[j, pl.ds(row, 256), :], act[1, q], (1, 0))

        def other_half():
            for q, j in units:
                csnd[p, q, j] = product(q, j, pl.multiple_of((1 - c) * 256, 256)).astype(BF)

        def own_half():
            for q, j in units:
                own[q, j] = product(q, j, pl.multiple_of(c * 256, 256))

        def mine(q, j, rel, half):
            row = pl.ds(pl.multiple_of(lax.rem(y + rel, 4) * 64 + half * 32, 32), 32)
            return own[q, j, row, :] + crcv[p, q, j, row, :].astype(F32)

        def first_sums():
            for q, j in units:
                for rel, half in ((2, 0), (2, 1), (1, 1), (3, 0)):
                    ysnd[p, q, j, rel - 1, half] = mine(q, j, rel, half).astype(BF)

        def relay_sums():
            for q, j in units:
                for rel, half in ((1, 0), (3, 1)):
                    total = mine(q, j, rel, half) + yrcv[p, q, j, 1, half].astype(F32)
                    ysnd[p, q, j, rel - 1, half] = total.astype(BF)

        def activate():
            for q, j in units:
                for half in range(2):
                    total = mine(q, j, 0, half)
                    total = total + yrcv[p, q, j, 0, half].astype(F32) + yrcv[p, q, j, 2, half].astype(F32)
                    keep = pl.ds(half * 32, 32)
                    if p == 0:
                        value, slope = gelu_parts(total)
                        deriv[q, j, keep, :] = slope
                    else:
                        value = total * deriv[q, j, keep, :]
                    row = pl.ds(pl.multiple_of(c * 256 + y * 64 + half * 32, 32), 32)
                    hid[p, q, j, row, :] = value.astype(BF)

        def piece(core, rel, first=0, rows=64):
            row = core * 256 + lax.rem(y + rel, 4) * 64 + first
            return hid.at[(*cut, pl.ds(pl.multiple_of(row, 32), rows))]

        n = lambda *rest: ("h", t) + rest
        plan.copy(n("c"), "c", csnd.at[cut], crcv.at[cut], crcv.at[cut])
        for rel, half, d in ((2, 0, "y+"), (2, 1, "y-"), (1, 1, "y+"), (3, 0, "y-"), (1, 0, "y+"), (3, 1, "y-")):
            src, dst = ysnd.at[(*cut, rel - 1, half)], yrcv.at[(*cut, rel - 1, half)]
            plan.copy(n("r", rel, half), d, src, dst, dst)
        plan.step(n("other"), [("act", p, q) for q in range(q0, q0 + nq)] + ["weights"], other_half, [n("c")])
        plan.step(n("own"), [n("other")], own_half)
        plan.step(n("first"), [n("own"), n("c")], first_sums, [n("r", 2, 0), n("r", 2, 1), n("r", 1, 1), n("r", 3, 0)])
        plan.step(n("relay"), [n("first"), n("r", 2, 0), n("r", 2, 1)], relay_sums, [n("r", 1, 0), n("r", 3, 1)])
        plan.copy(n("a", "+"), "y+", piece(c, 0), piece(c, 0), piece(c, 3))
        plan.copy(n("a", "-"), "y-", piece(c, 0), piece(c, 0), piece(c, 1))
        far = t in FAR_HIDDEN
        for sign, rel, first in (("+", 3, 0), ("-", 1, 32)):
            here = piece(c, 0 if far else rel, first, 32)
            plan.copy(n("f", sign), "y2" if far else "y" + sign, here, here, piece(c, 2, first, 32))
        for rel in range(4):
            plan.copy(n("k", rel), "c", piece(c, rel), piece(c, rel), piece(1 - c, rel))
        plan.step(n("act"), [n("relay")] + [n("r", *k) for k in ((1, 1), (3, 0), (1, 0), (3, 1))], activate, [n("a", "+"), n("a", "-")] + [n("f", "+"), n("f", "-")] * far + [n("k", 0)])
        if far:
            plan.step(n("pass"), [n(a, b) for a in "af" for b in "+-"], None, [n("k", 1), n("k", 3), n("k", 2)])
        else:
            plan.step(n("pass"), [n("a", "+"), n("a", "-")], None, [n("f", "+"), n("f", "-"), n("k", 1), n("k", 3)])
            plan.step(n("last"), [n("f", "+"), n("f", "-")], None, [n("k", 2)])
        plan.step(n("done"), [n("k", rel) for rel in range(4)], None)

    for t in range(len(TASKS)):
        hidden_task(t)

    def hidden_ready(p, keep):
        return [("h", t, "done") for t, task in enumerate(TASKS) if task[0] == p and keep(*task[1:])]

    def gradient(p, j):
        other = 1 - p
        slot = p * 3 + j

        def multiply():
            xtmp[...] = sum(dot(hid[p, q, j], act[other, q], (1, 1)) for q in range(4))
            for to in range(4):
                for half in range(2):
                    xsnd[slot, to, half] = xtmp[pl.ds(to * 128 + half * 64, 64), :].astype(BF)
            xown[slot] = xtmp[pl.ds(pl.multiple_of(x * 128, 128), 128), :]

        def relay_sums():
            for rel, half in ((1, 0), (3, 1)):
                to = lax.rem(x + rel, 4)
                total = xsnd[slot, to, half].astype(F32) + xrcv[slot, 1, half].astype(F32)
                xsnd[slot, to, half] = total.astype(BF)

        def finish():
            for half in range(2):
                rows = pl.ds(half * 64, 64)
                xown[slot, rows, :] = xown[slot, rows, :] + xrcv[slot, 0, half].astype(F32) + xrcv[slot, 2, half].astype(F32)
            if p == 0:
                gout_out[pl.ds(j * 128, 128), :] = xown[slot].astype(BF)
            else:
                gin_out[:, pl.ds(j * 128, 128)] = xown[slot].T.astype(BF)

        n = lambda *rest: ("w", p, j) + rest
        for rel, half, d in ((2, 0, "x+"), (2, 1, "x-"), (1, 1, "x+"), (3, 0, "x-"), (1, 0, "x+"), (3, 1, "x-")):
            there = xrcv.at[slot, rel - 1, half]
            plan.copy(n("r", rel, half), d, xsnd.at[slot, lax.rem(x + rel, 4), half], there, there)
        needs = [("act", other, q) for q in range(4)] + hidden_ready(p, lambda q0, nq, j0, nj: j0 <= j < j0 + nj)
        plan.step(n("mul"), needs, multiply, [n("r", 2, 0), n("r", 2, 1), n("r", 1, 1), n("r", 3, 0)])
        plan.step(n("relay"), [n("mul"), n("r", 2, 0), n("r", 2, 1)], relay_sums, [n("r", 1, 0), n("r", 3, 1)])
        plan.step(n("end"), [n("r", *k) for k in ((1, 1), (3, 0), (1, 0), (3, 1))], finish)

    for p in range(2):
        for j in range(3):
            gradient(p, j)

    def result(p, q0, nq):
        qs, cut = range(q0, q0 + nq), pl.ds(q0, nq)

        def multiply():
            for q in qs:
                if p == 0:
                    zacc[p, q] = sum(dot(w_out[j], hid[0, q, j], (0, 0)) for j in range(3))
                else:
                    zacc[p, q] = sum(dot(w_in[j], hid[1, q, j], (1, 0)) for j in range(3))

        def mine(q, rel, first=0, rows=192):
            at = lax.rem(z + rel + 8, 8)
            row = pl.multiple_of(lax.rem(at, 4) * 192 + first, 32)
            return zacc[p, q, pl.ds(row, rows), pl.ds(pl.multiple_of((at // 4) * 128, 128), 128)]

        def first():
            for q in qs:
                zsnd[p, q, 0, 0, pl.ds(0, 96), :] = mine(q, 4, 0, 96).astype(BF)
                zsnd[p, q, 1, 0, pl.ds(96, 96), :] = mine(q, 4, 96, 96).astype(BF)

        def add(s):
            def body():
                for q in qs:
                    for d, rel in ((0, 4 - s), (1, 4 + s)):
                        for half in range(2):
                            total = mine(q, rel, half * 96, 96)
                            rows = pl.ds(half * 96, 96)
                            if s > 1 or half == d:
                                total = total + zrcv[p, q, d, s - 1, rows, :].astype(F32)
                            zsnd[p, q, d, s, rows, :] = total.astype(BF)

            return body

        def first_far():
            first()
            for q in qs:
                for d, sign in ((0, 1), (1, -1)):
                    zsnd[p, q, d, 1] = mine(q, 3 * sign).astype(BF)
                    zsnd[p, q, d, 3] = mine(q, sign).astype(BF)

        def add_far():
            for q in qs:
                for d, sign in ((0, 1), (1, -1)):
                    for half in range(2):
                        rows = pl.ds(half * 96, 96)
                        total = mine(q, 2 * sign, half * 96, 96) + zrcv[p, q, d, 1, rows, :].astype(F32)
                        if half == d:
                            total = total + zrcv[p, q, d, 0, rows, :].astype(F32)
                        zsnd[p, q, d, 2, rows, :] = total.astype(BF)

        is_far = (p, q0) in FAR_SUMS

        def finish():
            for q in qs:
                total = mine(q, 0)
                for d in range(2):
                    total = total + zrcv[p, q, d, 3].astype(F32)
                    if is_far:
                        total = total + zrcv[p, q, d, 2].astype(F32)
                (mix_out, dtok_out)[p][:, pl.ds(q * 128, 128)] = total.astype(BF)

        n = lambda *rest: ("z", p, q0) + rest
        for d, link in ((0, "z+"), (1, "z-")):
            for s in range(4):
                rows = pl.ds(0, 192) if s else pl.ds(d * 96, 96)
                there = zrcv.at[p, cut, d, s, rows]
                way = link + link[1] if is_far and s in (0, 2) else link
                plan.copy(n("r", s, d), way, zsnd.at[p, cut, d, s, rows], there, there)
        needs = hidden_ready(p, lambda a0, na, j0, nj: a0 < q0 + nq and q0 < a0 + na)
        plan.step(n("mul"), needs, multiply)
        if is_far:
            plan.step(n(0), [n("mul")], first_far, [n("r", s, d) for s in (0, 1, 3) for d in range(2)])
            plan.step(n(1), [n("r", s, d) for s in (0, 1) for d in range(2)], add_far, [n("r", 2, 0), n("r", 2, 1)])
            plan.step(n("end"), [n("r", s, d) for s in (2, 3) for d in range(2)], finish)
            return
        plan.step(n(0), [n("mul")], first, [n("r", 0, 0), n("r", 0, 1)])
        for s in range(1, 4):
            plan.step(n(s), [n("r", s - 1, 0), n("r", s - 1, 1)], add(s), [n("r", s, 0), n("r", s, 1)])
        plan.step(n("end"), [n("r", 3, 0), n("r", 3, 1)], finish)

    for p in range(2):
        for q0, nq in SUMS[p]:
            result(p, q0, nq)

    index = {name: i for i, name in enumerate(plan.copies)}
    waited, sent = set(), []

    def remote(name, landing):
        link, src, dst, there = plan.copies[name]
        i = index[name]
        src, dst = (there, there) if landing else (src, dst)
        return pltpu.make_async_remote_copy(src, dst, send_sem.at[i], recv_sem.at[i], device_id=targets[link], device_id_type=MESH)

    for name in ORDER:
        needs, body, sends = plan.steps[name]
        for need in needs:
            if need in plan.copies and need not in waited:
                remote(need, True).wait_recv()
                waited.add(need)
        if body is not None:
            body()
        for copy in sends:
            remote(copy, False).start()
            sent.append(copy)
        while len(sent) > 40:
            remote(sent.pop(0), False).wait_send()
    for copy in sent:
        remote(copy, False).wait_send()


def copies_in_all():
    return 64 + 15 * len(TASKS) + 36 + 8 * sum(len(groups) for groups in SUMS)


def hand_over(*refs):
    for i in range(4):
        refs[4 + i][...] = refs[i][...]


def per_device(tokens, w_in, w_out, cotangent):
    vmem, far = pl.BlockSpec(memory_space=pltpu.VMEM), pl.BlockSpec(memory_space=pl.ANY)
    copies = copies_in_all()
    shapes = [jax.ShapeDtypeStruct(s, BF) for s in ((192, 512), (192, 512), (768, 384), (384, 768))]
    results = pl.pallas_call(
        kernel,
        out_shape=shapes,
        in_specs=[vmem, vmem, far, far],
        out_specs=[vmem] * 4,
        scratch_shapes=[
            pltpu.VMEM((2, 4, 768, 256), BF),
            pltpu.VMEM((3, 768, 512), BF),
            pltpu.VMEM((3, 512, 768), BF),
            pltpu.SemaphoreType.DMA((2, 3, 4)),
            pltpu.VMEM((2, 4, 3, 256, 256), BF),
            pltpu.VMEM((2, 4, 3, 256, 256), BF),
            pltpu.VMEM((4, 3, 256, 256), F32),
            pltpu.VMEM((2, 4, 3, 3, 2, 32, 256), BF),
            pltpu.VMEM((2, 4, 3, 3, 2, 32, 256), BF),
            pltpu.VMEM((4, 3, 64, 256), F32),
            pltpu.VMEM((2, 4, 3, 512, 256), BF),
            pltpu.VMEM((6, 4, 2, 64, 768), BF),
            pltpu.VMEM((6, 3, 2, 64, 768), BF),
            pltpu.VMEM((6, 128, 768), F32),
            pltpu.VMEM((512, 768), F32),
            pltpu.VMEM((2, 4, 768, 256), F32),
            pltpu.VMEM((2, 4, 2, 4, 192, 128), BF),
            pltpu.VMEM((2, 4, 2, 4, 192, 128), BF),
            pltpu.SemaphoreType.DMA((copies,)),
            pltpu.SemaphoreType.DMA((copies,)),
        ],
        compiler_params=pltpu.CompilerParams(
            collective_id=0, has_side_effects=True, vmem_limit_bytes=62 * 2**20
        ),
        cost_estimate=pl.CostEstimate(flops=14_500_000_000, bytes_accessed=12_000_000, transcendentals=400_000),
    )(tokens.T, cotangent.T, w_in, w_out)

    mixed, d_tokens, grad_in, grad_out = pl.pallas_call(
        hand_over,
        out_shape=shapes,
        in_specs=[vmem] * 4,
        out_specs=[vmem] * 4,
    )(*results)
    return (mixed.T, d_tokens.T, grad_in, grad_out)


def solution(mesh):
    split = Mesh(mesh.devices.reshape(2, 4, 4, 4, 2), ("zh", "x", "zl", "y", "c"))
    rows = P(("zh", "x"), ("y", "c", "zl"))
    return jax.shard_map(
        per_device,
        mesh=split,
        in_specs=(rows, P(("y", "c"), "zl"), P("zl", ("y", "c")), rows),
        out_specs=(rows, rows, P(("y", "c"), ("zl", "zh", "x")), P(("zl", "zh", "x"), ("y", "c"))),
        check_vma=False,
    )
```

time: 118 us -> 113 us (0.958)
  Pallas kernels: 117 us -> 112 us
    pallas_call x1, Pallas kernels: 114 us -> 110 us  [per_device(): pl.pallas_call(kernel, out_shape=shapes, in_specs=[vmem, vmem, far, far],...]
where the time goes in v3:
time: 113 us
  Pallas kernels  112 us (99%)
    pallas_call x1, Pallas kernels, per_device(): pl.pallas_call(kernel, out_shape=shapes, in_specs=[vmem, vmem, far, far],...  110 us
    pallas_call x1, Pallas kernels, per_device(): pl.pallas_call(hand_over, out_shape=shapes, in_specs=[vmem] * 4, out_spec...  2.6 us

profile of v3, /device:TPU:1, one launch (start us, length us, event | category | flops | bytes accessed | tf_op | source)
XLA Modules:
  0.0 112.9 jit_solution(11740222986886601640)
XLA Ops:
  0.6 109.7 %shard_map.75 = (bf16[192,512]{1,0:T(8,128)(2,1)}, bf16[192,512]{1,0:T(8,128)(2,1)}, bf16[768,384]{1,0:T(8,128)(2,1)}, bf16[384,768]{1,0:T(8,128)(2,1)}) custom-call(bf16[192,512]{1,0:T(8,128)(2,1)} %bitcast.4, bf16[192,512]{1,0:T(8,128)(2,1)} %bitcast.5, bf16[768,3072]{1,0:T(8,128)(2,1)} %w_in_hbm.1, bf16[3072,768]{1,0:T(8,128)(2,1)} %w_out_hbm.1), custom_call_target="tpu_custom_call" | custom-call | flops 14499999744 | bytes 12000000 | tf_op jit(solution)/shard_map/pallas_call | solution.py:597
  110.3 2.6 %shard_map.76 = (bf16[192,512]{1,0:T(8,128)(2,1)}, bf16[192,512]{1,0:T(8,128)(2,1)}, bf16[768,384]{1,0:T(8,128)(2,1)}, bf16[384,768]{1,0:T(8,128)(2,1)}) custom-call(bf16[192,512]{1,0:T(8,128)(2,1)} %get-tuple-element.12.refs_0_, bf16[192,512]{1,0:T(8,128)(2,1)} %get-tuple-element.13.refs_1_, bf16[768,384]{1,0:T(8,128)(2,1)} %get-tuple-element.14.refs_2_, ...), custom_call_target="tpu_custom_call" | custom-call | tf_op jit(solution)/shard_map/pallas_call | solution.py:630

commit v4 on v3

--- a/solution.py
+++ b/solution.py
@@ -32,219 +32,16 @@
 FAR_SUMS = ()
 FAR_HIDDEN = ()
 ORDER = (
-    ("g", 0, 1, 0),
-    ("g", 0, 0, 0),
-    ("g", 0, 3, 0),
-    ("g", 0, 1, 1),
-    ("g", 0, 2, 0),
-    ("g", 0, 0, 1),
-    ("g", 0, 1, 2),
-    ("g", 0, 2, 1),
-    ("g", 0, 3, 1),
-    "weights",
-    ("act", 0, 0),
-    ("h", 2, "other"),
-    ("h", 0, "other"),
-    ("h", 1, "other"),
-    ("g", 0, 1, 3),
-    ("h", 1, "own"),
-    ("g", 1, 2, 0),
-    ("h", 2, "own"),
-    ("h", 2, "first"),
-    ("h", 0, "own"),
-    ("g", 0, 2, 2),
-    ("h", 0, "first"),
-    ("g", 0, 3, 2),
-    ("g", 1, 3, 0),
-    ("h", 1, "first"),
-    ("act", 0, 1),
-    ("h", 5, "other"),
-    ("h", 3, "other"),
-    ("h", 2, "relay"),
-    ("h", 5, "own"),
-    ("g", 1, 0, 0),
-    ("h", 4, "other"),
-    ("h", 0, "relay"),
-    ("h", 5, "first"),
-    ("h", 4, "own"),
-    ("h", 3, "own"),
-    ("h", 1, "relay"),
-    ("g", 0, 2, 3),
-    ("h", 3, "first"),
-    ("g", 0, 3, 3),
-    ("g", 1, 2, 1),
-    ("h", 4, "first"),
-    ("h", 2, "act"),
-    ("g", 1, 3, 1),
-    ("h", 5, "relay"),
-    ("h", 0, "act"),
-    ("g", 1, 1, 0),
-    ("g", 1, 0, 1),
-    ("h", 1, "act"),
-    ("act", 0, 2),
-    ("h", 3, "relay"),
-    ("act", 0, 3),
-    ("h", 8, "other"),
-    ("h", 4, "relay"),
-    ("h", 6, "other"),
-    ("h", 8, "own"),
-    ("h", 2, "pass"),
-    ("h", 5, "act"),
-    ("g", 1, 2, 2),
-    ("h", 8, "first"),
-    ("g", 1, 3, 2),
-    ("h", 6, "own"),
-    ("h", 7, "other"),
-    ("h", 6, "first"),
-    ("g", 1, 1, 1),
-    ("g", 1, 0, 2),
-    ("h", 2, "last"),
-    ("h", 3, "act"),
-    ("h", 7, "own"),
-    ("h", 7, "first"),
-    ("g", 1, 2, 3),
-    ("h", 8, "relay"),
-    ("h", 0, "pass"),
-    ("g", 1, 3, 3),
-    ("h", 6, "relay"),
-    ("h", 5, "pass"),
-    ("g", 1, 1, 2),
-    ("h", 1, "pass"),
-    ("h", 7, "relay"),
-    ("g", 1, 0, 3),
-    ("act", 1, 2),
-    ("h", 4, "act"),
-    ("act", 1, 3),
-    ("h", 10, "other"),
-    ("h", 8, "act"),
-    ("h", 3, "pass"),
-    ("h", 0, "last"),
-    ("h", 6, "act"),
-    ("g", 1, 1, 3),
-    ("h", 14, "other"),
-    ("h", 14, "own"),
-    ("h", 7, "act"),
-    ("h", 5, "last"),
-    ("h", 1, "last"),
-    ("act", 1, 0),
-    ("h", 4, "pass"),
-    ("h", 2, "done"),
-    ("h", 10, "own"),
-    ("h", 14, "first"),
-    ("h", 12, "other"),
-    ("h", 8, "pass"),
-    ("act", 1, 1),
-    ("h", 11, "other"),
-    ("h", 13, "other"),
-    ("h", 5, "done"),
-    ("h", 6, "pass"),
-    ("h", 9, "other"),
-    ("h", 11, "own"),
-    ("h", 7, "pass"),
-    ("h", 10, "first"),
-    ("h", 13, "own"),
-    ("h", 14, "relay"),
-    ("h", 13, "first"),
-    ("h", 12, "own"),
-    ("h", 9, "own"),
-    ("h", 12, "first"),
-    ("h", 0, "done"),
-    ("h", 8, "last"),
-    ("h", 6, "last"),
-    ("h", 3, "last"),
-    ("h", 7, "last"),
-    ("h", 9, "first"),
-    ("h", 8, "done"),
-    ("h", 4, "last"),
-    ("w", 0, 2, "mul"),
-    ("h", 4, "done"),
-    ("h", 10, "relay"),
-    ("h", 7, "done"),
-    ("h", 6, "done"),
-    ("z", 0, 2, "mul"),
-    ("z", 0, 2, 0),
-    ("h", 13, "relay"),
-    ("h", 3, "done"),
-    ("h", 11, "first"),
-    ("h", 12, "relay"),
-    ("h", 14, "act"),
-    ("h", 1, "done"),
-    ("z", 0, 0, "mul"),
-    ("z", 0, 0, 0),
-    ("w", 0, 1, "mul"),
-    ("z", 0, 2, 1),
-    ("h", 13, "act"),
-    ("h", 9, "relay"),
-    ("h", 10, "act"),
-    ("w", 0, 0, "mul"),
-    ("h", 11, "relay"),
-    ("z", 0, 0, 1),
-    ("h", 14, "pass"),
-    ("h", 12, "act"),
-    ("w", 0, 1, "relay"),
-    ("h", 13, "pass"),
-    ("z", 0, 2, 2),
-    ("w", 0, 2, "relay"),
-    ("h", 9, "act"),
-    ("h", 11, "act"),
-    ("h", 10, "pass"),
-    ("z", 0, 0, 2),
-    ("h", 13, "last"),
-    ("h", 12, "pass"),
-    ("h", 14, "last"),
-    ("w", 0, 0, "relay"),
-    ("z", 0, 2, 3),
-    ("h", 9, "pass"),
-    ("h", 13, "done"),
-    ("h", 14, "done"),
-    ("w", 1, 2, "mul"),
-    ("h", 11, "pass"),
-    ("h", 10, "last"),
-    ("z", 0, 0, 3),
-    ("h", 12, "last"),
-    ("h", 9, "last"),
-    ("h", 10, "done"),
-    ("h", 12, "done"),
-    ("z", 1, 3, "mul"),
-    ("z", 1, 2, "mul"),
-    ("z", 1, 2, 0),
-    ("z", 1, 3, 0),
-    ("h", 11, "last"),
-    ("h", 9, "done"),
-    ("w", 1, 0, "mul"),
-    ("h", 11, "done"),
-    ("z", 1, 1, "mul"),
-    ("z", 1, 1, 0),
-    ("z", 1, 0, "mul"),
-    ("z", 1, 0, 0),
-    ("w", 1, 2, "relay"),
-    ("z", 1, 2, 1),
-    ("w", 0, 0, "end"),
-    ("z", 1, 3, 1),
-    ("w", 0, 2, "end"),
-    ("w", 1, 1, "mul"),
-    ("z", 1, 1, 1),
-    ("z", 1, 0, 1),
-    ("z", 0, 0, "end"),
-    ("w", 0, 1, "end"),
-    ("z", 1, 2, 2),
-    ("z", 1, 3, 2),
-    ("z", 1, 1, 2),
-    ("z", 1, 0, 2),
-    ("w", 1, 0, "relay"),
-    ("z", 1, 2, 3),
-    ("z", 1, 3, 3),
-    ("z", 0, 2, "end"),
-    ("w", 1, 1, "relay"),
-    ("z", 1, 1, 3),
-    ("z", 1, 0, 3),
-    ("z", 1, 2, "end"),
-    ("z", 1, 3, "end"),
-    ("z", 1, 1, "end"),
-    ("w", 1, 0, "end"),
-    ("w", 1, 2, "end"),
-    ("w", 1, 1, "end"),
-    ("z", 1, 0, "end"),
+    3, 0, 13, 4, 8, 1, 5, 9, 14, 38, 2, 55, 39, 47, 6, 48, 28, 56, 57, 40, 10, 41, 15, 33, 49, 7, 79, 63, 58,
+    80, 18, 71, 42, 81, 72, 64, 50, 11, 65, 16, 29, 73, 59, 34, 82, 43, 23, 19, 51, 12, 66, 17, 103, 74, 87,
+    104, 60, 83, 30, 105, 35, 88, 95, 89, 24, 20, 61, 67, 96, 97, 31, 106, 44, 36, 90, 84, 25, 52, 98, 21, 32,
+    75, 37, 119, 107, 68, 45, 91, 26, 151, 152, 99, 85, 53, 22, 76, 62, 120, 153, 135, 108, 27, 127, 143, 86,
+    92, 111, 128, 100, 121, 144, 154, 145, 136, 112, 137, 46, 109, 93, 69, 101, 113, 110, 77, 165, 78, 122,
+    102, 94, 183, 184, 146, 70, 129, 138, 155, 54, 177, 178, 162, 185, 147, 114, 123, 159, 130, 179, 156, 139,
+    163, 148, 186, 166, 115, 131, 124, 180, 149, 140, 157, 160, 187, 116, 150, 158, 174, 132, 125, 181, 141,
+    117, 126, 142, 207, 201, 202, 208, 133, 118, 168, 134, 195, 196, 189, 190, 175, 203, 161, 209, 167, 171,
+    197, 191, 182, 164, 204, 210, 198, 192, 169, 205, 211, 188, 172, 199, 193, 206, 212, 200, 170, 176, 173,
+    194,
 )
 
 
@@ -564,7 +361,9 @@
         src, dst = (there, there) if landing else (src, dst)
         return pltpu.make_async_remote_copy(src, dst, send_sem.at[i], recv_sem.at[i], device_id=targets[link], device_id_type=MESH)
 
-    for name in ORDER:
+    names = list(plan.steps)
+    for i in ORDER:
+        name = names[i]
         needs, body, sends = plan.steps[name]
         for need in needs:
             if need in plan.copies and need not in waited:

time: 113 us -> 113 us (level)
  no operation moved by 1% of the time
where the time goes in v4:
time: 113 us
  Pallas kernels  112 us (99%)
    pallas_call x1, Pallas kernels, per_device(): pl.pallas_call(kernel, out_shape=shapes, in_specs=[vmem, vmem, far, far],...  110 us
    pallas_call x1, Pallas kernels, per_device(): pl.pallas_call(hand_over, out_shape=shapes, in_specs=[vmem] * 4, out_spec...  2.6 us

profile of v4, /device:TPU:1, one launch (start us, length us, event | category | flops | bytes accessed | tf_op | source)
XLA Modules:
  0.0 112.9 jit_solution(11740222986886601640)
XLA Ops:
  0.6 109.7 %shard_map.75 = (bf16[192,512]{1,0:T(8,128)(2,1)}, bf16[192,512]{1,0:T(8,128)(2,1)}, bf16[768,384]{1,0:T(8,128)(2,1)}, bf16[384,768]{1,0:T(8,128)(2,1)}) custom-call(bf16[192,512]{1,0:T(8,128)(2,1)} %bitcast.4, bf16[192,512]{1,0:T(8,128)(2,1)} %bitcast.5, bf16[768,3072]{1,0:T(8,128)(2,1)} %w_in_hbm.1, bf16[3072,768]{1,0:T(8,128)(2,1)} %w_out_hbm.1), custom_call_target="tpu_custom_call" | custom-call | flops 14499999744 | bytes 12000000 | tf_op jit(solution)/shard_map/pallas_call | solution.py:396
  110.3 2.6 %shard_map.76 = (bf16[192,512]{1,0:T(8,128)(2,1)}, bf16[192,512]{1,0:T(8,128)(2,1)}, bf16[768,384]{1,0:T(8,128)(2,1)}, bf16[384,768]{1,0:T(8,128)(2,1)}) custom-call(bf16[192,512]{1,0:T(8,128)(2,1)} %get-tuple-element.12.refs_0_, bf16[192,512]{1,0:T(8,128)(2,1)} %get-tuple-element.13.refs_1_, bf16[768,384]{1,0:T(8,128)(2,1)} %get-tuple-element.14.refs_2_, ...), custom_call_target="tpu_custom_call" | custom-call | tf_op jit(solution)/shard_map/pallas_call | solution.py:429
